TPU v7x, 128 devices: a whole 4x4x4 slice. The times are simulated.
128 devices in a mesh: gx: 4 (over x), gy: 4 (over y), gz: 8 (over z, core).
Axes of the slice: x: 4, y: 4, z: 4, core: 2. Of those that a mesh axis runs over, the one named last changes fastest.
Arguments:
- functions: bfloat16 [10240, 8, 4096], P(('gx', 'gy', 'gz')), may hold values from -6 to 6
- responses: bfloat16 [10240, 8, 4096], P(('gx', 'gy', 'gz')), may hold values from -6 to 6
- box_domain: int32 [10240, 1], P(('gx', 'gy', 'gz')), may hold values from 0 to 127, as said below
- pair_index: int32 [2, 10240, 24], P(None, ('gx', 'gy', 'gz')), may hold values from 0 to 7
- pair_weight: float32 [10240, 24], P(('gx', 'gy', 'gz')), may hold values from -6 to 6
- kernel_xc: float32 [128, 8192], P(('gx', 'gy', 'gz')), may hold values from 0.25 to 2
Outputs:
- applied: bfloat16 [10240, 8, 4096], P(('gx', 'gy', 'gz'))
- potential: bfloat16 [128, 8192], P(('gx', 'gy', 'gz'))
Inputs may be any that keep to these rules, and one draw needn't show every extreme that they name: `box_domain`: boxes are held near their grid in y and z: a box of the device with mesh coordinates (ix, iy, iz) names domain ((ix + dx) mod 4, (iy + dy) mod 4, (iz + dz) mod 8) with dx in -2, -1, 0, dy in -1, 0 and dz in -1, 0, 1, and every device's boxes use all eighteen such offsets.
All inputs are finite; a program needn't handle non-finite values.
Results may differ from a plain program's by a relative error of at most 0.017.
Values may be sent and summed in bfloat16 or wider, within the bound.
No kernel may reach another device: no remote copies, remote signals or barrier semaphores. Data moves between devices by JAX's collectives and lax.ppermute only.
A program may use at most 128 MiB of HBM per device.

v0:
```python
import math

import jax
import jax.numpy as jnp
from jax import lax
from jax.sharding import PartitionSpec as P

HIGH = lax.Precision.HIGHEST


def interp_table(coarse):
    fine_len = 2 * coarse
    fine_pos = jnp.arange(fine_len, dtype=jnp.float32)[:, None]
    coarse_pos = jnp.arange(coarse, dtype=jnp.float32)[None, :]
    frequency = jnp.arange(1, coarse // 2, dtype=jnp.float32)[:, None, None]
    phases = 2.0 * jnp.pi * frequency * (fine_pos / fine_len - coarse_pos / coarse)
    summed = (
        1.0
        + 2.0 * jnp.sum(jnp.cos(phases), axis=0)
        + jnp.cos(jnp.pi * coarse_pos) * jnp.cos(jnp.pi * fine_pos * coarse / fine_len)
    )
    return (summed / coarse).astype(jnp.bfloat16)


def half_targets(domains, size_x, size_y, size_z):
    index_x = domains // (size_y * size_z)
    index_y = domains // size_z % size_y
    index_z = domains % size_z
    shift_x = jnp.array([0, 1], dtype=jnp.int32)
    return (
        (index_x[:, None] + shift_x[None, :]) % size_x * size_y + index_y[:, None]
    ) * size_z + index_z[:, None]


def interpolate(planes, table_full):
    box_count, fun_count, cells = planes.shape
    coarse = table_full.shape[1]
    shaped = planes.reshape(box_count, fun_count, coarse, coarse)
    stretched = jnp.einsum(
        "bfxy,Xx->bfyX", shaped, table_full, preferred_element_type=jnp.float32
    ).astype(jnp.bfloat16)
    return jnp.einsum(
        "bfyX,Yy->bfXY", stretched, table_full, preferred_element_type=jnp.float32
    ).astype(jnp.bfloat16)


def block_density(func_blk, resp_blk, pidx_blk, weight_blk, table_full):
    fun_count = func_blk.shape[1]
    coarse = table_full.shape[1]
    fine_f = interpolate(func_blk, table_full)
    fine_r = interpolate(resp_blk, table_full)
    levels = jnp.arange(fun_count, dtype=jnp.int32)
    first_hot = (pidx_blk[0][..., None] == levels).astype(jnp.float32)
    second_hot = (pidx_blk[1][..., None] == levels).astype(jnp.float32)
    kernel_pairs = jnp.einsum(
        "bp,bpf,bpg->bfg", weight_blk, first_hot, second_hot, precision=HIGH
    ).astype(jnp.bfloat16)
    mixed_resp = jnp.einsum(
        "bfg,bgXY->bfXY", kernel_pairs, fine_r, preferred_element_type=jnp.float32
    )
    density = jnp.sum(fine_f.astype(jnp.float32) * mixed_resp, axis=1)
    halves = density.reshape(density.shape[0], 2, 2 * coarse * coarse)
    return (halves, fine_f)


def block_apply(fine_f, box_pot, table_half):
    weighted = (box_pot[:, None].astype(jnp.float32) * fine_f.astype(jnp.float32)).astype(
        jnp.bfloat16
    )
    colwise = jnp.einsum(
        "bfXY,Xx->bfYx", weighted, table_half, preferred_element_type=jnp.float32
    ).astype(jnp.bfloat16)
    result = jnp.einsum(
        "bfYx,Yy->bfxy", colwise, table_half, preferred_element_type=jnp.float32
    ).astype(jnp.bfloat16)
    return result.reshape(result.shape[0], result.shape[1], result.shape[2] * result.shape[3])


def on_device(functions, responses, box_domain, pair_index, pair_weight, kernel_xc):
    box_count, fun_count, cells = functions.shape
    coarse = math.isqrt(cells)
    fine_side = 2 * coarse
    half_cells = coarse * fine_side
    table_full = interp_table(coarse)
    table_half = table_full * 0.5
    size_x = lax.axis_size("gx")
    size_y = lax.axis_size("gy")
    size_z = lax.axis_size("gz")
    devices = size_x * size_y * size_z
    per_block = 16
    blocks = box_count // per_block
    domains = box_domain[:, 0]
    targets = half_targets(domains, size_x, size_y, size_z)

    def blocked(array):
        return array.reshape((blocks, per_block) + array.shape[1:])

    pidx_blocks = pair_index.reshape(2, blocks, per_block, pair_index.shape[2]).transpose(
        1, 0, 2, 3
    )
    first_inputs = (blocked(functions), blocked(responses), pidx_blocks, blocked(pair_weight))

    def first_keep(inputs):
        return block_density(inputs[0], inputs[1], inputs[2], inputs[3], table_full)

    halves, fine_all = lax.map(first_keep, first_inputs)
    halves = halves.reshape(box_count * 2, half_cells)
    accumulated = jnp.zeros((devices, half_cells), jnp.float32).at[targets.reshape(-1)].add(halves)
    density = lax.psum_scatter(accumulated, ("gx", "gy", "gz"), scatter_dimension=0, tiled=True)
    potential = (kernel_xc * density).astype(jnp.bfloat16)
    all_potential = lax.all_gather(potential, ("gx", "gy", "gz"), axis=0, tiled=True)
    box_rows = all_potential[targets]
    box_pot = blocked(box_rows.reshape(box_count, fine_side, fine_side))

    def second_keep(inputs):
        return block_apply(inputs[0], inputs[1], table_half)

    applied = lax.map(second_keep, (fine_all, box_pot))
    return (applied.reshape(box_count, fun_count, cells), potential)


def solution(mesh):
    in_specs = (
        P(("gx", "gy", "gz"), None, None),
        P(("gx", "gy", "gz"), None, None),
        P(("gx", "gy", "gz"), None),
        P(None, ("gx", "gy", "gz"), None),
        P(("gx", "gy", "gz"), None),
        P(("gx", "gy", "gz"), None),
    )
    out_specs = (P(("gx", "gy", "gz"), None, None), P(("gx", "gy", "gz"), None))
    return jax.shard_map(
        on_device, mesh=mesh, in_specs=in_specs, out_specs=out_specs, check_vma=False
    )
```

profile of v0, /device:TPU:0, one launch (start us, length us, event | category | flops | bytes accessed | tf_op | source)
XLA Modules:
  0.0 494.6 jit_solution(2458690661498837029)
XLA Ops:
  10.4 3.3 cosine_reduce_fusion
  13.8 178.2 %while.22 = (s32[]{:T(128)}, f32[5,16,2,8192]{3,2,1,0:T(2,128)}, bf16[5,16,8,128,128]{4,3,2,1,0:T(8,128)(2,1)}, bf16[5,16,8,4096]{3,2,1,0:T(8,128)(2,1)}, bf16[1...) while((s32[]{:T(128)}, f32[5,16,2,8192]{3,2,1,0:T(2,128)}, ...), condition=%wide.region_3.4_spmd, body=%wide.region_1.3_spmd.sunk | while | flops 851486720 | bytes 53551720 | solution.py:106
  14.3 1.7 constant_dynamic-slice_fusion.3
  16.0 3.3 reshape.382
  19.2 2.3 convolution_convert_fusion.4
  21.6 3.6 copy.49
  25.2 7.9 %fusion.92 = f32[16,8,128,128]{3,1,2,0:T(8,128)} fusion(bf16[16,8,8,1]{2,1,3,0:T(8,128)(2,1)S(1)} %fusion.91, bf16[16,8,64,128]{2,1,3,0:T(8,128)(2,1)} %copy.49, bf16[128,64]{0,1:T(8,128)(2,1)S(1)} %get-tuple-element.258), kind=kOutput, calls=%fused_computation.5.clone.1 | convolution fusion | flops 304087040 | bytes 10504192 | tf_op jit(solution)/shard_map/while/body/eval_jaxpr/bfg,bgXY->bfXY/dot_general | solution.py:58
  33.1 2.3 reshape.383
  35.3 8.0 %fusion.93 = (f32[16,128,128]{2,1,0:T(8,128)S(1)}, bf16[16,8,128,128]{3,2,1,0:T(8,128)(2,1)}) fusion(f32[16,8,128,128]{3,1,2,0:T(8,128)} %fusion.92, bf16[128,64]{0,1:T(8,128)(2,1)S(1)} %get-tuple-element.258, bf16[16,8,64,64]{3,2,1,0:T(8,128)(2,1)S(1)} %reshape.383), kind=kOutput, calls=%fused_computation.3.clone.1 | convolution fusion | flops 411828224 | bytes 14696448 | tf_op jit(solution)/shard_map/while/body/eval_jaxpr/bfyX,Yy->bfXY/dot_general | solution.py:42
  43.3 4.7 bitcast_dynamic-update-slice_fusion.2
  49.9 1.7 constant_dynamic-slice_fusion.3
  51.5 3.3 reshape.382
  54.8 2.3 convolution_convert_fusion.4
  57.2 3.6 copy.49
  60.8 7.9 %fusion.92 = f32[16,8,128,128]{3,1,2,0:T(8,128)} fusion(bf16[16,8,8,1]{2,1,3,0:T(8,128)(2,1)S(1)} %fusion.91, bf16[16,8,64,128]{2,1,3,0:T(8,128)(2,1)} %copy.49, bf16[128,64]{0,1:T(8,128)(2,1)S(1)} %get-tuple-element.258), kind=kOutput, calls=%fused_computation.5.clone.1 | convolution fusion | flops 304087040 | bytes 10504192 | tf_op jit(solution)/shard_map/while/body/eval_jaxpr/bfg,bgXY->bfXY/dot_general | solution.py:58
  68.6 2.3 reshape.383
  70.9 8.0 %fusion.93 = (f32[16,128,128]{2,1,0:T(8,128)S(1)}, bf16[16,8,128,128]{3,2,1,0:T(8,128)(2,1)}) fusion(f32[16,8,128,128]{3,1,2,0:T(8,128)} %fusion.92, bf16[128,64]{0,1:T(8,128)(2,1)S(1)} %get-tuple-element.258, bf16[16,8,64,64]{3,2,1,0:T(8,128)(2,1)S(1)} %reshape.383), kind=kOutput, calls=%fused_computation.3.clone.1 | convolution fusion | flops 411828224 | bytes 14696448 | tf_op jit(solution)/shard_map/while/body/eval_jaxpr/bfyX,Yy->bfXY/dot_general | solution.py:42
  78.9 4.7 bitcast_dynamic-update-slice_fusion.2
  85.5 1.7 constant_dynamic-slice_fusion.3
  87.2 3.3 reshape.382
  90.5 2.3 convolution_convert_fusion.4
  92.8 3.6 copy.49
  96.4 7.9 %fusion.92 = f32[16,8,128,128]{3,1,2,0:T(8,128)} fusion(bf16[16,8,8,1]{2,1,3,0:T(8,128)(2,1)S(1)} %fusion.91, bf16[16,8,64,128]{2,1,3,0:T(8,128)(2,1)} %copy.49, bf16[128,64]{0,1:T(8,128)(2,1)S(1)} %get-tuple-element.258), kind=kOutput, calls=%fused_computation.5.clone.1 | convolution fusion | flops 304087040 | bytes 10504192 | tf_op jit(solution)/shard_map/while/body/eval_jaxpr/bfg,bgXY->bfXY/dot_general | solution.py:58
  104.3 2.3 reshape.383
  106.6 8.0 %fusion.93 = (f32[16,128,128]{2,1,0:T(8,128)S(1)}, bf16[16,8,128,128]{3,2,1,0:T(8,128)(2,1)}) fusion(f32[16,8,128,128]{3,1,2,0:T(8,128)} %fusion.92, bf16[128,64]{0,1:T(8,128)(2,1)S(1)} %get-tuple-element.258, bf16[16,8,64,64]{3,2,1,0:T(8,128)(2,1)S(1)} %reshape.383), kind=kOutput, calls=%fused_computation.3.clone.1 | convolution fusion | flops 411828224 | bytes 14696448 | tf_op jit(solution)/shard_map/while/body/eval_jaxpr/bfyX,Yy->bfXY/dot_general | solution.py:42
  114.5 4.7 bitcast_dynamic-update-slice_fusion.2
  121.1 1.7 constant_dynamic-slice_fusion.3
  122.8 3.3 reshape.382
  126.1 2.3 convolution_convert_fusion.4
  128.4 3.6 copy.49
  132.0 7.9 %fusion.92 = f32[16,8,128,128]{3,1,2,0:T(8,128)} fusion(bf16[16,8,8,1]{2,1,3,0:T(8,128)(2,1)S(1)} %fusion.91, bf16[16,8,64,128]{2,1,3,0:T(8,128)(2,1)} %copy.49, bf16[128,64]{0,1:T(8,128)(2,1)S(1)} %get-tuple-element.258), kind=kOutput, calls=%fused_computation.5.clone.1 | convolution fusion | flops 304087040 | bytes 10504192 | tf_op jit(solution)/shard_map/while/body/eval_jaxpr/bfg,bgXY->bfXY/dot_general | solution.py:58
  139.9 2.3 reshape.383
  142.2 8.0 %fusion.93 = (f32[16,128,128]{2,1,0:T(8,128)S(1)}, bf16[16,8,128,128]{3,2,1,0:T(8,128)(2,1)}) fusion(f32[16,8,128,128]{3,1,2,0:T(8,128)} %fusion.92, bf16[128,64]{0,1:T(8,128)(2,1)S(1)} %get-tuple-element.258, bf16[16,8,64,64]{3,2,1,0:T(8,128)(2,1)S(1)} %reshape.383), kind=kOutput, calls=%fused_computation.3.clone.1 | convolution fusion | flops 411828224 | bytes 14696448 | tf_op jit(solution)/shard_map/while/body/eval_jaxpr/bfyX,Yy->bfXY/dot_general | solution.py:42
  150.1 4.7 bitcast_dynamic-update-slice_fusion.2
  156.7 1.7 constant_dynamic-slice_fusion.3
  158.4 3.3 reshape.382
  161.7 2.3 convolution_convert_fusion.4
  164.0 3.6 copy.49
  167.6 7.9 %fusion.92 = f32[16,8,128,128]{3,1,2,0:T(8,128)} fusion(bf16[16,8,8,1]{2,1,3,0:T(8,128)(2,1)S(1)} %fusion.91, bf16[16,8,64,128]{2,1,3,0:T(8,128)(2,1)} %copy.49, bf16[128,64]{0,1:T(8,128)(2,1)S(1)} %get-tuple-element.258), kind=kOutput, calls=%fused_computation.5.clone.1 | convolution fusion | flops 304087040 | bytes 10504192 | tf_op jit(solution)/shard_map/while/body/eval_jaxpr/bfg,bgXY->bfXY/dot_general | solution.py:58
  175.5 2.3 reshape.383
  177.8 8.0 %fusion.93 = (f32[16,128,128]{2,1,0:T(8,128)S(1)}, bf16[16,8,128,128]{3,2,1,0:T(8,128)(2,1)}) fusion(f32[16,8,128,128]{3,1,2,0:T(8,128)} %fusion.92, bf16[128,64]{0,1:T(8,128)(2,1)S(1)} %get-tuple-element.258, bf16[16,8,64,64]{3,2,1,0:T(8,128)(2,1)S(1)} %reshape.383), kind=kOutput, calls=%fused_computation.3.clone.1 | convolution fusion | flops 411828224 | bytes 14696448 | tf_op jit(solution)/shard_map/while/body/eval_jaxpr/bfyX,Yy->bfXY/dot_general | solution.py:42
  185.7 4.7 bitcast_dynamic-update-slice_fusion.2
  192.1 7.7 %reshape.367 = f32[160,8192]{1,0:T(8,128)} reshape(f32[5,16,2,8192]{3,2,1,0:T(2,128)} %get-tuple-element.72) | data formatting | bytes 10485760 | tf_op jit(solution)/shard_map/reshape | solution.py:107
  199.8 11.0 %scatter_custom_fusion = f32[128,8192]{1,0:T(8,128)} fusion(s32[160]{0:T(256)S(1)} %bitcast.120, f32[160,8192]{1,0:T(8,128)} %reshape.367, f32[]{:T(128)} %constant.113.clone.1), kind=kCustom, calls=%fused_computation.46 | custom fusion | flops 1310720 | bytes 4194816 | tf_op jit(solution)/shard_map/scatter-add | solution.py:108
  210.8 156.7 %all-reduce.3.cloned.1.call-done = f32[128,8192]{1,0:T(8,128)} async-done(((f32[128,8192]{1,0:T(8,128)}), f32[128,8192]{1,0:T(8,128)}) %all-reduce.3.cloned.1.call-update) | async-done | bytes 4194320
  367.5 1.6 fusion.51
  369.4 67.1 %all-gather.3.cloned.1.call-done = bf16[128,1,8192]{2,1,0:T(2,128)(2,1)} async-done(((bf16[1,1,8192]{2,1,0:T(2,128)(2,1)}), bf16[128,1,8192]{2,1,0:T(2,128)(2,1)}) %all-gather.3.cloned.1.call-update) | async-done | bytes 2097168 | tf_op jit(solution)/shard_map/all_gather | solution.py:111
  436.5 4.5 copy.45
  440.9 3.8 gather_fusion
  444.7 5.3 %reshape_reshape.3 = bf16[5,16,128,128]{3,2,1,0:T(8,128)(2,1)} reshape(bf16[160,8192]{1,0:T(8,128)(2,1)} %gather_fusion) | data formatting | bytes 5242880 | tf_op jit(solution)/shard_map/reshape;reshape | solution.py:96
  449.9 37.8 %while.23 = (s32[]{:T(128)}, bf16[5,16,8,4096]{3,2,1,0:T(8,128)(2,1)}, bf16[5,16,128,128]{3,2,1,0:T(8,128)(2,1)}, bf16[5,16,8,128,128]{4,3,2,1,0:T(8,128)(2,1)}, bf16[128,64]{0,1:T(8,128)(2,1)S(1)}, /*index=5*/s32[]{:T(128)}) while((s32[]{:T(128)}, bf16[5,16,8,4096]{3,2,1,0:T(8,128)(2,1)}, bf16[5,16,128,128]{3,2,1,0:T(8,128)(2,1)}, ...), condition=%wide.region_7.8_spmd, body=%wide.region_6.7_spmd.sunk | while | flops 410779648 | bytes 12092489 | solution.py:118
  449.9 1.1 bitcast_convert_fusion.2
  451.1 3.7 fusion.98
  454.8 1.7 broadcast_in_dim.46
  457.5 1.1 bitcast_convert_fusion.2
  458.6 3.7 fusion.98
  462.3 1.7 broadcast_in_dim.46
  466.2 3.7 fusion.98
  469.9 1.7 broadcast_in_dim.46
  473.8 3.7 fusion.98
  477.5 1.7 broadcast_in_dim.46
  480.2 1.1 bitcast_convert_fusion.2
  481.3 3.7 fusion.98
  485.0 1.7 broadcast_in_dim.46
  (66 shorter events, 20.3 us)
Async XLA Ops:
  7.2 360.3 %all-reduce.3.cloned.1.call-start = ((), (), s32[]{:S(2)}) async-start(), calls=%async_computation.1 | async-start | bytes 8388608
  199.8 167.7 %copy-start = (f32[1,8192]{1,0:T(1,128)S(1)}, f32[1,8192]{1,0:T(1,128)}, u32[]{:S(2)}) copy-start(f32[1,8192]{1,0:T(1,128)} %param.16) | copy-start | bytes 98308
  210.8 225.7 %all-gather.3.cloned.1.call-start = ((), (), s32[]{:S(2)}) async-start(), calls=%async_computation | async-start | bytes 4227072 | tf_op jit(solution)/shard_map/all_gather | solution.py:111
Sparse Core Ops, SparseCore 0:
  210.9 156.5 all-reduce.2
  371.2 65.1 all-gather.2
where the time goes:
time: 497 us; the launch traced here: 495 us
  waiting for transfers between devices  224 us (45%)
  local copies, waits for them, and re-layouts  123 us (25%)
  matrix products  110 us (22%)
  other arithmetic  22.7 us (5%)
  between operations  14.1 us (3%)
    unnamed x3, waiting for transfers between devices  157 us
    all_gather x1, waiting for transfers between devices, on_device(): lax.all_gather(potential, ('gx', 'gy', 'gz'), axis=0, tiled=True)  67.1 us
    dot_general x5, matrix products, interpolate(): jnp.einsum('bfyX,Yy->bfXY', stretched, table_full, preferred_element_type...  39.8 us
    dot_general x5, matrix products, block_density(): jnp.einsum('bfg,bgXY->bfXY', kernel_pairs, fine_r, preferred_element_type...  39.4 us
    dynamic_update_slice x10, local copies, waits for them, and re-layouts, on_device(): halves, fine_all = lax.map(first_keep, first_inputs)  28.9 us
    reshape x10, local copies, waits for them, and re-layouts, interpolate(): shaped = planes.reshape(box_count, fun_count, coarse, coarse)  27.8 us
    dot_general x5, matrix products, block_apply(): jnp.einsum('bfYx,Yy->bfxy', colwise, table_half, preferred_element_type=j...  18.4 us
    convert_element_type x5, local copies, waits for them, and re-layouts, interpolate(): stretched = jnp.einsum('bfxy,Xx->bfyX', shaped, table_full, preferred_ele...  18.1 us
  transfers between devices with their start and end apart: 2, of which 2 were waited for; matrix products, arithmetic and copies ran while one was open for 0% of the time, Pallas kernels for 0%

commit v1 on v0

v1 whole, which is shorter than its diff:
```python
import jax
import jax.numpy as jnp
import ml_dtypes
import numpy as np
from jax import lax
from jax.experimental import pallas as pl
from jax.experimental.pallas import tpu as pltpu
from jax.sharding import PartitionSpec as P

AXES = ("gx", "gy", "gz")
GROUP = 8
VMEM_LIMIT = 60 * 1024 * 1024
BF16 = jnp.bfloat16
F32 = jnp.float32


def tables():
    m = (2.0 * np.arange(64) + 1.0)[:, None]
    n = np.arange(64.0)[None, :]
    k = np.arange(1, 32)[:, None, None]
    total = 1.0 + 2.0 * np.cos(2.0 * np.pi * k * (m / 128 - n / 64)).sum(0)
    total = total + np.cos(np.pi * n) * np.cos(np.pi * m / 2)
    odd = (total / 64).astype(ml_dtypes.bfloat16)
    x_of = np.concatenate([np.arange(0, 64, 2), np.arange(1, 64, 2)])
    odd_x = odd[x_of][:, x_of]
    wide = np.zeros((256, 256), ml_dtypes.bfloat16)
    for i in range(4):
        wide[64 * i : 64 * i + 64, 64 * i : 64 * i + 64] = odd.T
    return odd_x, wide


def cell_orders():
    rows = np.zeros((64, 64), np.float32)
    for par in range(2):
        for p in range(2):
            for c in range(16):
                rows[4 * c + 2 * p + par, (par * 2 + p) * 16 + c] = 1
    cols = np.zeros((128, 128), np.float32)
    for par in range(2):
        for y in range(64):
            cols[par * 64 + y, 2 * y + par] = 1
    return rows, cols


def lane_low(shape):
    return lax.broadcasted_iota(jnp.int32, shape, len(shape) - 1) % 128 < 64


def slots_of(at, domain):
    box_x = lax.div(domain, 32)
    slot_y = lax.rem(lax.rem(lax.div(domain, 8), 4) - at[0] + 5, 4)
    slot_z = lax.rem(lax.rem(domain, 8) - at[1] + 9, 8)
    base = (slot_z * 2 + slot_y) * 4
    return base + box_x, base + lax.rem(box_x + 1, 4)


def density_kernel(at, domains, func, resp, pidx, pw, spread, odd_x, wide, part, fine, acc, stage, mixer, rs):
    step = pl.program_id(0)
    rows8 = 8 * GROUP

    @pl.when(step == 0)
    def _():
        acc[...] = jnp.zeros_like(acc)

        def widen(a, precision=None):
            return jnp.dot(a, spread[...], precision=precision, preferred_element_type=F32)

        level = (lax.broadcasted_iota(jnp.int32, (24, 640), 1) % 8).astype(F32)
        one = jnp.ones((24, 640), F32)
        weight = widen(pw[...], lax.Precision.HIGHEST)
        first = jnp.where(widen(pidx[0].astype(F32)) == level, weight, 0.0)
        second = jnp.where(widen(pidx[1].astype(F32)) == level, one, 0.0)
        at_row = lax.broadcasted_iota(jnp.int32, (128, 128), 0) // 8
        at_col = lax.broadcasted_iota(jnp.int32, (128, 128), 1) // 8
        for i in range(5):
            cut = slice(128 * i, 128 * i + 128)
            cross = lax.dot_general(
                first[:, cut],
                second[:, cut],
                (((0,), (0,)), ((), ())),
                precision=lax.Precision.HIGHEST,
                preferred_element_type=F32,
            )
            cross = jnp.where(at_row == at_col, cross, 0.0).astype(BF16)
            for j in range(128 // rows8):
                cut = slice(rows8 * j, rows8 * j + rows8)
                mixer[128 // rows8 * i + j] = cross[cut, cut]

    low = lane_low((32, 128))
    mixed = jnp.dot(mixer[step], resp[...].reshape(rows8, 4096), preferred_element_type=F32)
    for b in range(GROUP):
        for c in range(32):
            stage[0, b, 8 * c : 8 * c + 8, :] = func[b, :, 128 * c : 128 * c + 128].astype(F32)
            stage[1, b, 8 * c : 8 * c + 8, :] = mixed[8 * b : 8 * b + 8, 128 * c : 128 * c + 128]

    def place(which, b):
        return fine.at[b, 0] if which == 0 else rs.at[b]

    for b in range(GROUP):
        for which in range(2):
            to = place(which, b)
            for h in range(4):
                one = stage[which, b, pl.ds(2 * h, 32, stride=8), :]
                two = stage[which, b, pl.ds(2 * h + 1, 32, stride=8), :]
                p0 = jnp.where(low, one, pltpu.roll(two, 64, 1)).astype(BF16)
                p1 = jnp.where(low, pltpu.roll(one, 64, 1), two).astype(BF16)
                row, lane = 128 * (h // 2), 128 * (h % 2)
                to[row : row + 32, lane : lane + 128] = p0
                to[row + 32 : row + 64, lane : lane + 128] = p1
    for b in range(GROUP):
        for which in range(2):
            to = place(which, b)
            for i in range(2):
                even = to[128 * i : 128 * i + 64, :]
                odd = jnp.dot(odd_x[...], even, preferred_element_type=F32)
                to[128 * i + 64 : 128 * i + 128, :] = odd.astype(BF16)
    for b in range(GROUP):
        tall_f = fine[b, 0]
        tall_r = rs[b]
        shift_f = jnp.dot(tall_f, wide[...], preferred_element_type=F32)
        shift_r = jnp.dot(tall_r, wide[...], preferred_element_type=F32)
        fine[b, 1] = shift_f.astype(BF16)
        den_e = tall_f.astype(F32) * tall_r.astype(F32)
        den_o = shift_f * shift_r
        s0, s1 = slots_of(at, domains[step * GROUP + b])
        for par, den in ((0, den_e), (1, den_o)):
            den = den[:128] + den[128:]
            den = den[:, :128] + den[:, 128:]
            for g in range(4):
                acc[s0, par, 16 * g : 16 * g + 16] += den[32 * g : 32 * g + 16]
                acc[s1, par, 16 * g : 16 * g + 16] += den[32 * g + 16 : 32 * g + 32]

    @pl.when(step == pl.num_programs(0) - 1)
    def _():
        lowd = lane_low((64, 128))

        def fold(d, _):
            sums = [acc[d, par] + pltpu.roll(acc[d, par], 64, 1) for par in range(2)]
            part[d] = jnp.where(lowd, sums[0], sums[1]).astype(BF16)
            return 0

        lax.fori_loop(0, 24, fold, 0)


def box_density(at, domains, functions, responses, pair_index, pair_weight):
    boxes = functions.shape[0]
    odd_x, wide = tables()
    steps = boxes // GROUP
    spread = np.repeat(np.eye(boxes, dtype=np.float32), 8, axis=1)
    return pl.pallas_call(
        density_kernel,
        grid_spec=pltpu.PrefetchScalarGridSpec(
            num_scalar_prefetch=2,
            grid=(steps,),
            in_specs=[
                pl.BlockSpec((GROUP, 8, 4096), lambda i, *_: (i, 0, 0)),
                pl.BlockSpec((GROUP, 8, 4096), lambda i, *_: (i, 0, 0)),
                pl.BlockSpec((2, 24, boxes), lambda i, *_: (0, 0, 0)),
                pl.BlockSpec((24, boxes), lambda i, *_: (0, 0)),
                pl.BlockSpec((boxes, 8 * boxes), lambda i, *_: (0, 0)),
                pl.BlockSpec((64, 64), lambda i, *_: (0, 0)),
                pl.BlockSpec((256, 256), lambda i, *_: (0, 0)),
            ],
            out_specs=[
                pl.BlockSpec((24, 64, 128), lambda i, *_: (0, 0, 0)),
                pl.BlockSpec((GROUP, 2, 256, 256), lambda i, *_: (i, 0, 0, 0)),
            ],
            scratch_shapes=[
                pltpu.VMEM((24, 2, 64, 128), F32),
                pltpu.VMEM((2, GROUP, 256, 128), F32),
                pltpu.VMEM((steps, 8 * GROUP, 8 * GROUP), BF16),
                pltpu.VMEM((GROUP, 256, 256), BF16),
            ],
        ),
        out_shape=[
            jax.ShapeDtypeStruct((24, 64, 128), BF16),
            jax.ShapeDtypeStruct((boxes, 2, 256, 256), BF16),
        ],
        compiler_params=pltpu.CompilerParams(vmem_limit_bytes=VMEM_LIMIT),
        cost_estimate=pl.CostEstimate(flops=2 * 10**9, bytes_accessed=32 * 10**6, transcendentals=0),
        name="box_density",
    )(
        at,
        domains,
        functions,
        responses,
        jnp.transpose(pair_index, (0, 2, 1)),
        jnp.transpose(pair_weight, (1, 0)),
        jnp.asarray(spread),
        jnp.asarray(odd_x),
        jnp.asarray(wide),
    )


def apply_kernel(at, domains, pot, fine, odd_xt, wide_t, out, twice, stage, col):
    step = pl.program_id(0)

    @pl.when(step == 0)
    def _():
        lowd = lane_low((64, 128))

        def double(d, _):
            own = pot[d].astype(F32) * 0.25
            other = pltpu.roll(own, 64, 1)
            twice[d, 0] = jnp.where(lowd, own, other).astype(BF16)
            twice[d, 1] = jnp.where(lowd, other, own).astype(BF16)
            return 0

        lax.fori_loop(0, 24, double, 0)

    low = lane_low((32, 128))
    for b in range(GROUP):
        s0, s1 = slots_of(at, domains[step * GROUP + b])
        weighted = []
        for par in range(2):
            pieces = []
            for g in range(4):
                pieces.append(twice[s0, par, 16 * g : 16 * g + 16])
                pieces.append(twice[s1, par, 16 * g : 16 * g + 16])
            level = jnp.concatenate(pieces, axis=0)
            level = jnp.concatenate([level, level], axis=1)
            level = jnp.concatenate([level, level], axis=0)
            weighted.append(level * fine[b, par])
        col[b] = weighted[0].astype(F32) + jnp.dot(weighted[1], wide_t[...], preferred_element_type=F32)
    for b in range(GROUP):
        for i in range(2):
            odd = col[b, 128 * i + 64 : 128 * i + 128].astype(BF16)
            res = col[b, 128 * i : 128 * i + 64] + jnp.dot(odd_xt[...], odd, preferred_element_type=F32)
            for k in range(2):
                p0 = res[:32, 128 * k : 128 * k + 128]
                p1 = res[32:, 128 * k : 128 * k + 128]
                f = 4 * i + 2 * k
                stage[b, pl.ds(f, 32, stride=8), :] = jnp.where(low, p0, pltpu.roll(p1, 64, 1))
                stage[b, pl.ds(f + 1, 32, stride=8), :] = jnp.where(low, pltpu.roll(p0, 64, 1), p1)
    for b in range(GROUP):
        for c in range(32):
            out[b, :, 128 * c : 128 * c + 128] = stage[b, 8 * c : 8 * c + 8, :].astype(BF16)


def box_apply(at, domains, pot, fine):
    boxes = fine.shape[0]
    odd_x, wide = tables()
    steps = boxes // GROUP
    return pl.pallas_call(
        apply_kernel,
        grid_spec=pltpu.PrefetchScalarGridSpec(
            num_scalar_prefetch=2,
            grid=(steps,),
            in_specs=[
                pl.BlockSpec((24, 64, 128), lambda i, *_: (0, 0, 0)),
                pl.BlockSpec((GROUP, 2, 256, 256), lambda i, *_: (i, 0, 0, 0)),
                pl.BlockSpec((64, 64), lambda i, *_: (0, 0)),
                pl.BlockSpec((256, 256), lambda i, *_: (0, 0)),
            ],
            out_specs=pl.BlockSpec((GROUP, 8, 4096), lambda i, *_: (i, 0, 0)),
            scratch_shapes=[
                pltpu.VMEM((24, 2, 64, 128), BF16),
                pltpu.VMEM((GROUP, 256, 128), F32),
                pltpu.VMEM((GROUP, 256, 256), F32),
            ],
        ),
        out_shape=jax.ShapeDtypeStruct((boxes, 8, 4096), BF16),
        compiler_params=pltpu.CompilerParams(vmem_limit_bytes=VMEM_LIMIT),
        cost_estimate=pl.CostEstimate(flops=10**9, bytes_accessed=27 * 10**6, transcendentals=0),
        name="box_apply",
    )(at, domains, pot, fine, jnp.asarray(np.ascontiguousarray(odd_x.T)), jnp.asarray(np.ascontiguousarray(wide.T)))


def permuted(rows, cols, a, back):
    at_row, at_col = (1, 0) if back else (0, 1)
    high = lax.Precision.HIGHEST
    a = lax.dot_general(rows[...], a, (((at_row,), (0,)), ((), ())), precision=high, preferred_element_type=F32)
    return lax.dot_general(a, cols[...], (((1,), (at_col,)), ((), ())), precision=high, preferred_element_type=F32)


def store_kernel(kxc, rows, cols, out):
    exact = permuted(rows, cols, kxc[...], False)
    out[0] = exact.astype(BF16)
    out[1] = (exact - out[0].astype(F32)).astype(BF16)


def natural_kernel(at_x, pot, rows, cols, out):
    out[...] = permuted(rows, cols, pot[at_x[0]].astype(F32), True).astype(BF16)


def small_call(kernel, scalars, arrays, shape, name):
    smem, vmem = pl.BlockSpec(memory_space=pltpu.SMEM), pl.BlockSpec(memory_space=pltpu.VMEM)
    return pl.pallas_call(
        kernel,
        in_specs=[smem] * len(scalars) + [vmem] * (len(arrays) + 2),
        out_specs=vmem,
        out_shape=jax.ShapeDtypeStruct(shape, BF16),
        cost_estimate=pl.CostEstimate(flops=10**7, bytes_accessed=10**6, transcendentals=0),
        name=name,
    )(*scalars, *arrays, *(jnp.asarray(o) for o in cell_orders()))


def shifted(array, axis, by):
    size = lax.axis_size(axis)
    return lax.ppermute(array, axis, [(i, (i + by) % size) for i in range(size)])


def on_device(functions, responses, box_domain, pair_index, pair_weight, kernel_xc):
    at_x, at_y, at_z = (lax.axis_index(a) for a in AXES)
    at = jnp.stack([at_y, at_z])
    domains = box_domain.reshape(-1)
    part, fine = box_density(at, domains, functions, responses, pair_index, pair_weight)
    kxc = small_call(store_kernel, (), (kernel_xc.reshape(64, 128),), (2, 64, 128), "kernel_order")

    part = part.reshape(3, 2, 4, 64, 128)
    lower = shifted(part[0], "gz", -1)
    upper = shifted(part[2], "gz", 1)
    by_z = (part[1].astype(F32) + lower.astype(F32) + upper.astype(F32)).astype(BF16)
    by_y = (by_z[1].astype(F32) + shifted(by_z[0], "gy", -1).astype(F32)).astype(BF16)
    sent = jnp.concatenate([by_y, kxc])
    got = [sent] + [shifted(sent, "gx", s) for s in (1, 2, 3)]
    total = sum(g[:4].astype(F32) for g in got)
    pot = []
    for x in range(4):
        which = (at_x - x) % 4
        high, low = (lax.select_n(which, *(g[k] for g in got)).astype(F32) for k in (4, 5))
        pot.append((total[x] * (high + low)).astype(BF16))
    pot = jnp.stack(pot)
    by_y = jnp.stack([shifted(pot, "gy", 1), pot])
    natural = small_call(natural_kernel, (at_x.reshape(1),), (pot,), (64, 128), "natural_order")
    by_z = jnp.stack([shifted(by_y, "gz", 1), by_y, shifted(by_y, "gz", -1)]).reshape(24, 64, 128)
    applied = box_apply(at, domains, by_z, fine)
    return applied, natural.reshape(1, 8192)


def solution(mesh):
    spec3, spec2 = P(AXES, None, None), P(AXES, None)
    return jax.shard_map(
        on_device,
        mesh=mesh,
        in_specs=(spec3, spec3, spec2, P(None, AXES, None), spec2, spec2),
        out_specs=(spec3, spec2),
        check_vma=False,
    )
```

time: 497 us -> 86.9 us (0.17)
  waiting for transfers between devices: 224 us -> 16.5 us
  local copies, waits for them, and re-layouts: 123 us -> 2.42 us
  matrix products: 110 us -> 0 us
  Pallas kernels: 0 us -> 47.3 us
  other arithmetic: 22.7 us -> 5.4 us
  between operations: 14.1 us -> 0.7 us
  starting transfers between devices: 0.08 us -> 13.4 us
    unnamed x3 -> x0, waiting for transfers between devices: 157 us -> none
    dot_general x25 -> x0, matrix products: 110 us -> none  [the longest x5 39.8 us: interpolate(): jnp.einsum('bfyX,Yy->bfXY', stretched, table_full, preferred_element_type...]
    all_gather x1 -> x0, waiting for transfers between devices: 67.1 us -> none  [on_device(): lax.all_gather(potential, ('gx', 'gy', 'gz'), axis=0, tiled=True)]
    pallas_call x0 -> x4, Pallas kernels: none -> 47.3 us  [the longest x1 25.4 us: box_density(): pl.pallas_call(density_kernel, grid_spec=pltpu.PrefetchScalarGridSpec(num...]
    reshape x11 -> x0, local copies, waits for them, and re-layouts: 35.4 us -> none  [the longest x10 27.8 us: interpolate(): shaped = planes.reshape(box_count, fun_count, coarse, coarse)]
    dynamic_update_slice x15 -> x0, local copies, waits for them, and re-layouts: 34.1 us -> none  [the longest x10 28.9 us: on_device(): halves, fine_all = lax.map(first_keep, first_inputs)]
    convert_element_type x5 -> x0, local copies, waits for them, and re-layouts: 18.1 us -> none  [interpolate(): stretched = jnp.einsum('bfxy,Xx->bfyX', shaped, table_full, preferred_ele...]
    ppermute x0 -> x9, waiting for transfers between devices: none -> 16.5 us  [shifted(): lax.ppermute(array, axis, [(i, (i + by) % size) for i in range(size)])]
  transfers between devices with their start and end apart: 2 -> 9, of which waited for: 2 -> 6; matrix products, arithmetic and copies ran while one was open for 0% -> 2% of each run, Pallas kernels for 0% -> 4%
where the time goes in v1:
time: 86.9 us; the launch traced here: 85.7 us
  Pallas kernels  47.3 us (54%)
  waiting for transfers between devices  16.5 us (19%)
  starting transfers between devices  13.4 us (15%)
  other arithmetic  5.4 us (6%)
  local copies, waits for them, and re-layouts  2.42 us (3%)
    pallas_call x1, Pallas kernels, box_density(): pl.pallas_call(density_kernel, grid_spec=pltpu.PrefetchScalarGridSpec(num...  25.4 us
    pallas_call x1, Pallas kernels, box_apply(): pl.pallas_call(apply_kernel, grid_spec=pltpu.PrefetchScalarGridSpec(num_s...  18 us
    ppermute x9, waiting for transfers between devices, shifted(): lax.ppermute(array, axis, [(i, (i + by) % size) for i in range(size)])  16.5 us
    ppermute x9, starting transfers between devices, shifted(): lax.ppermute(array, axis, [(i, (i + by) % size) for i in range(size)])  13.4 us
    pallas_call x2, Pallas kernels, small_call(): pl.pallas_call(kernel, in_specs=[smem] * len(scalars) + [vmem] * (len(arr...  3.82 us
    convert_element_type x4, other arithmetic, on_device(): pot.append((total[x] * (high + low)).astype(BF16))  3.03 us
  transfers between devices with their start and end apart: 9, of which 6 were waited for; matrix products, arithmetic and copies ran while one was open for 2% of the time, Pallas kernels for 4%

profile of v1, /device:TPU:0, one launch (start us, length us, event | category | flops | bytes accessed | tf_op | source)
XLA Modules:
  0.0 85.7 jit_solution(18380693482463061656)
XLA Ops:
  0.6 0.6 pad_add_fusion.at
  1.3 25.4 %box_density.1 = (bf16[24,64,128]{2,1,0:T(8,128)(2,1)}, bf16[80,2,256,256]{3,2,1,0:T(8,128)(2,1)}) custom-call(s32[2]{0:T(128)} %pad_add_fusion.at, s32[80]{0:T(128)} %bitcast.43, bf16[80,8,4096]{2,1,0:T(8,128)(2,1)} %func.1, bf16[80,8,4096]{2,1,0:T(8,128)(2,1)} %resp.1, s32[2,24,80]{2,1,0:T(8,128)} %bitcast.41, f32[24,80]{1,0:T(8,128)} %bitcast.42, ...), custom_call_target="tpu_custom_call" | custom-call | flops 2000000000 | bytes 32000000 | tf_op jit(solution)/shard_map/box_density/pallas_call | solution.py:150
  26.7 1.1 %fusion.9 = (bf16[8,64,128]{2,1,0:T(8,128)(2,1)S(1)}, bf16[8,64,128]{2,1,0:T(8,128)(2,1)S(1)}, bf16[8,64,128]{2,1,0:T(8,128)(2,1)S(1)}) fusion(bf16[24,64,128]{2,1,0:T(8,128)(2,1)} %get-tuple-element.4), kind=kLoop, calls=%fused_computation.24 | loop fusion | bytes 786432 | tf_op jit(solution)/shard_map/slice | solution.py:311
  27.8 0.0 collective-permute-start.1
  27.8 3.6 %collective-permute-start = (bf16[2,4,64,128]{3,2,1,0:T(8,128)(2,1)S(1)}, bf16[2,4,64,128]{3,2,1,0:T(8,128)(2,1)S(1)}, u32[]{:S(2)}, u32[]{:S(2)}) collective-permute-start(bf16[2,4,64,128]{3,2,1,0:T(8,128)(2,1)S(1)} %bitcast.35), channel_id=1, source_target_pairs={{0,7},{1,0},{2,1},{3,2},{4,3},{5,4},{6,5},{7,6},{8,15},{9,8},{10,9... | collective-permute-start | bytes 393224 | tf_op jit(solution)/shard_map/ppermute | solution.py:300
  31.4 2.6 %collective-permute-done.1 = bf16[2,4,64,128]{3,2,1,0:T(8,128)(2,1)S(1)} collective-permute-done((bf16[2,4,64,128]{3,2,1,0:T(8,128)(2,1)S(1)}, bf16[2,4,64,128]{3,2,1,0:T(8,128)(2,1)S(1)}, u32[]{:S(2)}, u32[]{:S(2)}) %collective-permute-start.1) | collective-permute-done | bytes 131104 | tf_op jit(solution)/shard_map/ppermute | solution.py:300
  34.0 0.0 collective-permute-done
  34.0 0.1 fusion.1
  34.1 3.1 %collective-permute-start.2 = (bf16[4,64,128]{2,1,0:T(8,128)(2,1)S(1)}, bf16[4,64,128]{2,1,0:T(8,128)(2,1)S(1)}, u32[]{:S(2)}, u32[]{:S(2)}) collective-permute-start(bf16[4,64,128]{2,1,0:T(8,128)(2,1)S(1)} %slice_bitcast_fusion), channel_id=1, source_target_pairs={{0,24},{8,0},{16,8},{24,16},{1,25},{9,1},{17,9},{25,17},{2,26},{10... | collective-permute-start | bytes 196616 | tf_op jit(solution)/shard_map/ppermute | solution.py:300
  37.2 2.0 %kernel_order.1 = bf16[2,64,128]{2,1,0:T(8,128)(2,1)} custom-call(f32[64,128]{1,0:T(8,128)} %bitcast.39, f32[64,64]{1,0:T(8,128)} %constant.65.clone.rows, f32[128,128]{1,0:T(8,128)} %constant.66.clone.cols), custom_call_target="tpu_custom_call" | custom-call | flops 10000000 | bytes 1000000 | tf_op jit(solution)/shard_map/kernel_order/pallas_call | solution.py:288
  39.1 0.0 collective-permute-done.2
  39.2 0.8 pad_maximum_fusion.2
  39.9 2.8 %collective-permute-start.5 = (bf16[6,64,128]{2,1,0:T(8,128)(2,1)S(1)}, bf16[6,64,128]{2,1,0:T(8,128)(2,1)S(1)}, u32[]{:S(2)}, u32[]{:S(2)}) collective-permute-start(bf16[6,64,128]{2,1,0:T(8,128)(2,1)S(1)} %pad_maximum_fusion.2), channel_id=1, source_target_pairs={{0,96},{32,0},{64,32},{96,64},{1,97},{33,1},{65,33},{97,65},{2,98}... | collective-permute-start | bytes 294920 | tf_op jit(solution)/shard_map/ppermute | solution.py:300
  42.8 0.8 collective-permute-start.4
  43.6 0.9 %collective-permute-start.3 = (bf16[6,64,128]{2,1,0:T(8,128)(2,1)S(1)}, bf16[6,64,128]{2,1,0:T(8,128)(2,1)S(1)}, u32[]{:S(2)}, u32[]{:S(2)}) collective-permute-start(bf16[6,64,128]{2,1,0:T(8,128)(2,1)S(1)} %pad_maximum_fusion.2), channel_id=1, source_target_pairs={{0,32},{32,64},{64,96},{96,0},{1,33},{33,65},{65,97},{97,1},{2,34}... | collective-permute-start | bytes 294920 | tf_op jit(solution)/shard_map/ppermute | solution.py:300
  44.4 2.7 %collective-permute-done.5 = bf16[6,64,128]{2,1,0:T(8,128)(2,1)S(1)} collective-permute-done((bf16[6,64,128]{2,1,0:T(8,128)(2,1)S(1)}, bf16[6,64,128]{2,1,0:T(8,128)(2,1)S(1)}, u32[]{:S(2)}, u32[]{:S(2)}) %collective-permute-start.5) | collective-permute-done | bytes 98336 | tf_op jit(solution)/shard_map/ppermute | solution.py:300
  47.1 2.6 %collective-permute-done.4 = bf16[6,64,128]{2,1,0:T(8,128)(2,1)S(1)} collective-permute-done((bf16[6,64,128]{2,1,0:T(8,128)(2,1)S(1)}, bf16[6,64,128]{2,1,0:T(8,128)(2,1)S(1)}, u32[]{:S(2)}, u32[]{:S(2)}) %collective-permute-start.4) | collective-permute-done | bytes 98336 | tf_op jit(solution)/shard_map/ppermute | solution.py:300
  49.8 1.0 %collective-permute-done.3 = bf16[6,64,128]{2,1,0:T(8,128)(2,1)S(1)} collective-permute-done((bf16[6,64,128]{2,1,0:T(8,128)(2,1)S(1)}, bf16[6,64,128]{2,1,0:T(8,128)(2,1)S(1)}, u32[]{:S(2)}, u32[]{:S(2)}) %collective-permute-start.3) | collective-permute-done | bytes 98336 | tf_op jit(solution)/shard_map/ppermute | solution.py:300
  50.8 0.8 fusion.3
  51.6 0.8 fusion.4
  52.4 0.8 fusion.5
  53.1 0.8 fusion.6
  53.9 0.0 copy-start
  53.9 0.4 collective-permute-start.6
  54.3 5.2 %collective-permute-done.6 = bf16[4,64,128]{2,1,0:T(8,128)(2,1)S(1)} collective-permute-done((bf16[4,64,128]{2,1,0:T(8,128)(2,1)S(1)}, bf16[4,64,128]{2,1,0:T(8,128)(2,1)S(1)}, u32[]{:S(2)}, u32[]{:S(2)}) %collective-permute-start.6) | collective-permute-done | bytes 65568 | tf_op jit(solution)/shard_map/ppermute | solution.py:300
  59.5 1.8 %collective-permute-start.8 = (bf16[2,4,64,128]{3,2,1,0:T(8,128)(2,1)S(1)}, bf16[2,4,64,128]{3,2,1,0:T(8,128)(2,1)S(1)}, u32[]{:S(2)}, u32[]{:S(2)}) collective-permute-start(bf16[2,4,64,128]{3,2,1,0:T(8,128)(2,1)S(1)} %get-tuple-element.10), channel_id=1, source_target_pairs={{0,7},{1,0},{2,1},{3,2},{4,3},{5,4},{6,5},{7,6},{8,15},{9,8},{10,9... | collective-permute-start | bytes 393224 | tf_op jit(solution)/shard_map/ppermute | solution.py:300
  61.3 0.0 collective-permute-start.7
  61.3 0.0 copy-done
  61.3 1.8 %natural_order.1 = bf16[64,128]{1,0:T(8,128)(2,1)} custom-call(s32[1]{0:T(128)} %bitcast.17.at_x, bf16[4,64,128]{2,1,0:T(8,128)(2,1)} %copy-done, f32[64,64]{1,0:T(8,128)} %constant.65.clone.rows, f32[128,128]{1,0:T(8,128)} %constant.66.clone.cols), custom_call_target="tpu_custom_call" | custom-call | flops 10000000 | bytes 1000000 | tf_op jit(solution)/shard_map/natural_order/pallas_call | solution.py:288
  63.2 1.4 %copy.19 = bf16[1,1,64,128]{3,1,2,0:T(2,128)(2,1)} copy(bf16[1,1,64,128]{3,2,1,0:T(8,128)(2,1)} %bitcast.38) | data formatting | bytes 32768
  64.5 0.0 collective-permute-done.8
  64.5 2.4 %collective-permute-done.7 = bf16[2,4,64,128]{3,2,1,0:T(8,128)(2,1)S(1)} collective-permute-done((bf16[2,4,64,128]{3,2,1,0:T(8,128)(2,1)S(1)}, bf16[2,4,64,128]{3,2,1,0:T(8,128)(2,1)S(1)}, u32[]{:S(2)}, u32[]{:S(2)}) %collective-permute-start.7) | collective-permute-done | bytes 131104 | tf_op jit(solution)/shard_map/ppermute | solution.py:300
  66.9 0.8 pad_maximum_fusion
  67.7 18.0 %box_apply.1 = bf16[80,8,4096]{2,1,0:T(8,128)(2,1)} custom-call(s32[2]{0:T(128)} %pad_add_fusion.at, s32[80]{0:T(128)} %bitcast.44, bf16[24,64,128]{2,1,0:T(8,128)(2,1)} %bitcast.31, bf16[80,2,256,256]{3,2,1,0:T(8,128)(2,1)} %get-tuple-element.5.fine, bf16[64,64]{1,0:T(8,128)(2,1)} %constant.67.clone.odd_xt, bf16[256,256]{1,0:T(8,128)(2,1)} %constant.68.clone.wide_t), custom_call_target="tpu_custom_call" | custom-call | flops 1000000000 | bytes 27000000 | tf_op jit(solution)/shard_map/box_apply/pallas_call | solution.py:244
  (5 shorter events, 0.1 us)
Async XLA Ops:
  27.8 6.2 %collective-permute-start.1 = (bf16[2,4,64,128]{3,2,1,0:T(8,128)(2,1)S(1)}, bf16[2,4,64,128]{3,2,1,0:T(8,128)(2,1)S(1)}, u32[]{:S(2)}, u32[]{:S(2)}) collective-permute-start(bf16[2,4,64,128]{3,2,1,0:T(8,128)(2,1)S(1)} %bitcast.36), channel_id=1, source_target_pairs={{0,1},{1,2},{2,3},{3,4},{4,5},{5,6},{6,7},{7,0},{8,9},{9,10},{10,1... | collective-permute-start | bytes 393224 | tf_op jit(solution)/shard_map/ppermute | solution.py:300
  27.8 6.2 %collective-permute-start = (bf16[2,4,64,128]{3,2,1,0:T(8,128)(2,1)S(1)}, bf16[2,4,64,128]{3,2,1,0:T(8,128)(2,1)S(1)}, u32[]{:S(2)}, u32[]{:S(2)}) collective-permute-start(bf16[2,4,64,128]{3,2,1,0:T(8,128)(2,1)S(1)} %bitcast.35), channel_id=1, source_target_pairs={{0,7},{1,0},{2,1},{3,2},{4,3},{5,4},{6,5},{7,6},{8,15},{9,8},{10,9... | collective-permute-start | bytes 393224 | tf_op jit(solution)/shard_map/ppermute | solution.py:300
  34.1 5.1 %collective-permute-start.2 = (bf16[4,64,128]{2,1,0:T(8,128)(2,1)S(1)}, bf16[4,64,128]{2,1,0:T(8,128)(2,1)S(1)}, u32[]{:S(2)}, u32[]{:S(2)}) collective-permute-start(bf16[4,64,128]{2,1,0:T(8,128)(2,1)S(1)} %slice_bitcast_fusion), channel_id=1, source_target_pairs={{0,24},{8,0},{16,8},{24,16},{1,25},{9,1},{17,9},{25,17},{2,26},{10... | collective-permute-start | bytes 196616 | tf_op jit(solution)/shard_map/ppermute | solution.py:300
  39.9 7.2 %collective-permute-start.5 = (bf16[6,64,128]{2,1,0:T(8,128)(2,1)S(1)}, bf16[6,64,128]{2,1,0:T(8,128)(2,1)S(1)}, u32[]{:S(2)}, u32[]{:S(2)}) collective-permute-start(bf16[6,64,128]{2,1,0:T(8,128)(2,1)S(1)} %pad_maximum_fusion.2), channel_id=1, source_target_pairs={{0,96},{32,0},{64,32},{96,64},{1,97},{33,1},{65,33},{97,65},{2,98}... | collective-permute-start | bytes 294920 | tf_op jit(solution)/shard_map/ppermute | solution.py:300
  42.8 7.0 %collective-permute-start.4 = (bf16[6,64,128]{2,1,0:T(8,128)(2,1)S(1)}, bf16[6,64,128]{2,1,0:T(8,128)(2,1)S(1)}, u32[]{:S(2)}, u32[]{:S(2)}) collective-permute-start(bf16[6,64,128]{2,1,0:T(8,128)(2,1)S(1)} %pad_maximum_fusion.2), channel_id=1, source_target_pairs={{0,64},{32,96},{64,0},{96,32},{1,65},{33,97},{65,1},{97,33},{2,66}... | collective-permute-start | bytes 294920 | tf_op jit(solution)/shard_map/ppermute | solution.py:300
  43.6 7.3 %collective-permute-start.3 = (bf16[6,64,128]{2,1,0:T(8,128)(2,1)S(1)}, bf16[6,64,128]{2,1,0:T(8,128)(2,1)S(1)}, u32[]{:S(2)}, u32[]{:S(2)}) collective-permute-start(bf16[6,64,128]{2,1,0:T(8,128)(2,1)S(1)} %pad_maximum_fusion.2), channel_id=1, source_target_pairs={{0,32},{32,64},{64,96},{96,0},{1,33},{33,65},{65,97},{97,1},{2,34}... | collective-permute-start | bytes 294920 | tf_op jit(solution)/shard_map/ppermute | solution.py:300
  53.9 7.4 %copy-start = (bf16[4,64,128]{2,1,0:T(8,128)(2,1)}, bf16[4,64,128]{2,1,0:T(8,128)(2,1)S(1)}, u32[]{:S(2)}) copy-start(bf16[4,64,128]{2,1,0:T(8,128)(2,1)S(1)} %get-tuple-element.11.pot) | copy-start | bytes 196612
  53.9 5.5 %collective-permute-start.6 = (bf16[4,64,128]{2,1,0:T(8,128)(2,1)S(1)}, bf16[4,64,128]{2,1,0:T(8,128)(2,1)S(1)}, u32[]{:S(2)}, u32[]{:S(2)}) collective-permute-start(bf16[4,64,128]{2,1,0:T(8,128)(2,1)S(1)} %get-tuple-element.11.pot), channel_id=1, source_target_pairs={{0,8},{8,16},{16,24},{24,0},{1,9},{9,17},{17,25},{25,1},{2,10},{10... | collective-permute-start | bytes 196616 | tf_op jit(solution)/shard_map/ppermute | solution.py:300
  59.5 5.0 %collective-permute-start.8 = (bf16[2,4,64,128]{3,2,1,0:T(8,128)(2,1)S(1)}, bf16[2,4,64,128]{3,2,1,0:T(8,128)(2,1)S(1)}, u32[]{:S(2)}, u32[]{:S(2)}) collective-permute-start(bf16[2,4,64,128]{3,2,1,0:T(8,128)(2,1)S(1)} %get-tuple-element.10), channel_id=1, source_target_pairs={{0,7},{1,0},{2,1},{3,2},{4,3},{5,4},{6,5},{7,6},{8,15},{9,8},{10,9... | collective-permute-start | bytes 393224 | tf_op jit(solution)/shard_map/ppermute | solution.py:300
  61.3 5.6 %collective-permute-start.7 = (bf16[2,4,64,128]{3,2,1,0:T(8,128)(2,1)S(1)}, bf16[2,4,64,128]{3,2,1,0:T(8,128)(2,1)S(1)}, u32[]{:S(2)}, u32[]{:S(2)}) collective-permute-start(bf16[2,4,64,128]{3,2,1,0:T(8,128)(2,1)S(1)} %get-tuple-element.10), channel_id=1, source_target_pairs={{0,1},{1,2},{2,3},{3,4},{4,5},{5,6},{6,7},{7,0},{8,9},{9,10},{10,1... | collective-permute-start | bytes 393224 | tf_op jit(solution)/shard_map/ppermute | solution.py:300

commit v2 on v1

--- a/solution.py
+++ b/solution.py
@@ -8,8 +8,8 @@
 from jax.sharding import PartitionSpec as P
 
 AXES = ("gx", "gy", "gz")
-GROUP = 8
-VMEM_LIMIT = 60 * 1024 * 1024
+GROUP = 16
+LAG = 1
 BF16 = jnp.bfloat16
 F32 = jnp.float32
 
@@ -54,7 +54,14 @@
     return base + box_x, base + lax.rem(box_x + 1, 4)
 
 
-def density_kernel(at, domains, func, resp, pidx, pw, spread, odd_x, wide, part, fine, acc, stage, mixer, rs):
+def in_turn(stages, lag=LAG):
+    for t in range(GROUP + lag * (len(stages) - 1)):
+        for i, stage in enumerate(stages):
+            if 0 <= t - lag * i < GROUP:
+                stage(t - lag * i)
+
+
+def density_kernel(at, domains, func, resp, pidx, pw, spread, odd_x, wide, part0, part1, part2, fine, acc, stage, mixer, rs):
     step = pl.program_id(0)
     rows8 = 8 * GROUP
 
@@ -66,12 +73,12 @@
             return jnp.dot(a, spread[...], precision=precision, preferred_element_type=F32)
 
         level = (lax.broadcasted_iota(jnp.int32, (24, 640), 1) % 8).astype(F32)
-        one = jnp.ones((24, 640), F32)
         weight = widen(pw[...], lax.Precision.HIGHEST)
         first = jnp.where(widen(pidx[0].astype(F32)) == level, weight, 0.0)
-        second = jnp.where(widen(pidx[1].astype(F32)) == level, one, 0.0)
-        at_row = lax.broadcasted_iota(jnp.int32, (128, 128), 0) // 8
-        at_col = lax.broadcasted_iota(jnp.int32, (128, 128), 1) // 8
+        second = jnp.where(widen(pidx[1].astype(F32)) == level, 1.0, 0.0)
+        at_row = lax.broadcasted_iota(jnp.int32, (128, 128), 0)
+        at_col = lax.broadcasted_iota(jnp.int32, (128, 128), 1)
+        cycle = jnp.where(at_row % 8 == at_col % 8, 1.0, 0.0).astype(BF16)
         for i in range(5):
             cut = slice(128 * i, 128 * i + 128)
             cross = lax.dot_general(
@@ -81,22 +88,28 @@
                 precision=lax.Precision.HIGHEST,
                 preferred_element_type=F32,
             )
-            cross = jnp.where(at_row == at_col, cross, 0.0).astype(BF16)
-            for j in range(128 // rows8):
-                cut = slice(rows8 * j, rows8 * j + rows8)
-                mixer[128 // rows8 * i + j] = cross[cut, cut]
+            cross = jnp.where(at_row // 8 == at_col // 8, cross, 0.0).astype(BF16)
+            mixer[cut] = jnp.dot(cross, cycle, preferred_element_type=F32)
 
     low = lane_low((32, 128))
-    mixed = jnp.dot(mixer[step], resp[...].reshape(rows8, 4096), preferred_element_type=F32)
-    for b in range(GROUP):
-        for c in range(32):
-            stage[0, b, 8 * c : 8 * c + 8, :] = func[b, :, 128 * c : 128 * c + 128].astype(F32)
-            stage[1, b, 8 * c : 8 * c + 8, :] = mixed[8 * b : 8 * b + 8, 128 * c : 128 * c + 128]
+    on_block = (
+        lax.broadcasted_iota(jnp.int32, (16, 8, 128), 0) == lax.broadcasted_iota(jnp.int32, (16, 8, 128), 2) // 8
+    )
 
     def place(which, b):
         return fine.at[b, 0] if which == 0 else rs.at[b]
 
-    for b in range(GROUP):
+    def mix(b):
+        pairs = mixer[pl.ds(pl.multiple_of((step * GROUP + b) * 8, 8), 8), :]
+        pairs = jnp.where(on_block, jnp.broadcast_to(pairs[None], (16, 8, 128)), 0.0)
+        pairs = pairs.reshape(128, 128).astype(BF16)
+        raw = jnp.concatenate([resp[b, :128], resp[b, 128:]], axis=1)
+        mixed = jnp.dot(pairs, raw, preferred_element_type=F32)
+        stage[0, b] = func[b].astype(F32)
+        stage[1, b, :128] = mixed[:, :128]
+        stage[1, b, 128:] = mixed[:, 128:]
+
+    def regroup(b):
         for which in range(2):
             to = place(which, b)
             for h in range(4):
@@ -107,14 +120,16 @@
                 row, lane = 128 * (h // 2), 128 * (h % 2)
                 to[row : row + 32, lane : lane + 128] = p0
                 to[row + 32 : row + 64, lane : lane + 128] = p1
-    for b in range(GROUP):
+
+    def along_x(b):
         for which in range(2):
             to = place(which, b)
             for i in range(2):
                 even = to[128 * i : 128 * i + 64, :]
                 odd = jnp.dot(odd_x[...], even, preferred_element_type=F32)
                 to[128 * i + 64 : 128 * i + 128, :] = odd.astype(BF16)
-    for b in range(GROUP):
+
+    def along_y(b):
         tall_f = fine[b, 0]
         tall_r = rs[b]
         shift_f = jnp.dot(tall_f, wide[...], preferred_element_type=F32)
@@ -130,16 +145,24 @@
                 acc[s0, par, 16 * g : 16 * g + 16] += den[32 * g : 32 * g + 16]
                 acc[s1, par, 16 * g : 16 * g + 16] += den[32 * g + 16 : 32 * g + 32]
 
+    in_turn((mix, regroup, along_x, along_y))
+
     @pl.when(step == pl.num_programs(0) - 1)
     def _():
         lowd = lane_low((64, 128))
 
         def fold(d, _):
             sums = [acc[d, par] + pltpu.roll(acc[d, par], 64, 1) for par in range(2)]
-            part[d] = jnp.where(lowd, sums[0], sums[1]).astype(BF16)
-            return 0
-
-        lax.fori_loop(0, 24, fold, 0)
+            to = (part0, part1, part2)[d // 8]
+            to[d % 8] = jnp.where(lowd, sums[0], sums[1]).astype(BF16)
+
+        for d in range(24):
+            fold(d, 0)
+
+
+def as_tiles(array):
+    boxes = array.shape[0]
+    return array.reshape(boxes, 8, 32, 128).transpose(0, 2, 1, 3).reshape(boxes, 256, 128)
 
 
 def box_density(at, domains, functions, responses, pair_index, pair_weight):
@@ -153,8 +176,8 @@
             num_scalar_prefetch=2,
             grid=(steps,),
             in_specs=[
-                pl.BlockSpec((GROUP, 8, 4096), lambda i, *_: (i, 0, 0)),
-                pl.BlockSpec((GROUP, 8, 4096), lambda i, *_: (i, 0, 0)),
+                pl.BlockSpec((GROUP, 256, 128), lambda i, *_: (i, 0, 0)),
+                pl.BlockSpec((GROUP, 256, 128), lambda i, *_: (i, 0, 0)),
                 pl.BlockSpec((2, 24, boxes), lambda i, *_: (0, 0, 0)),
                 pl.BlockSpec((24, boxes), lambda i, *_: (0, 0)),
                 pl.BlockSpec((boxes, 8 * boxes), lambda i, *_: (0, 0)),
@@ -162,28 +185,28 @@
                 pl.BlockSpec((256, 256), lambda i, *_: (0, 0)),
             ],
             out_specs=[
-                pl.BlockSpec((24, 64, 128), lambda i, *_: (0, 0, 0)),
+                *[pl.BlockSpec((8, 64, 128), lambda i, *_: (0, 0, 0))] * 3,
                 pl.BlockSpec((GROUP, 2, 256, 256), lambda i, *_: (i, 0, 0, 0)),
             ],
             scratch_shapes=[
                 pltpu.VMEM((24, 2, 64, 128), F32),
                 pltpu.VMEM((2, GROUP, 256, 128), F32),
-                pltpu.VMEM((steps, 8 * GROUP, 8 * GROUP), BF16),
+                pltpu.VMEM((8 * boxes, 128), F32),
                 pltpu.VMEM((GROUP, 256, 256), BF16),
             ],
         ),
         out_shape=[
-            jax.ShapeDtypeStruct((24, 64, 128), BF16),
+            *[jax.ShapeDtypeStruct((8, 64, 128), BF16)] * 3,
             jax.ShapeDtypeStruct((boxes, 2, 256, 256), BF16),
         ],
-        compiler_params=pltpu.CompilerParams(vmem_limit_bytes=VMEM_LIMIT),
+        compiler_params=pltpu.CompilerParams(vmem_limit_bytes=60 * 1024 * 1024),
         cost_estimate=pl.CostEstimate(flops=2 * 10**9, bytes_accessed=32 * 10**6, transcendentals=0),
         name="box_density",
     )(
         at,
         domains,
-        functions,
-        responses,
+        as_tiles(functions),
+        as_tiles(responses),
         jnp.transpose(pair_index, (0, 2, 1)),
         jnp.transpose(pair_weight, (1, 0)),
         jnp.asarray(spread),
@@ -206,10 +229,11 @@
             twice[d, 1] = jnp.where(lowd, other, own).astype(BF16)
             return 0
 
-        lax.fori_loop(0, 24, double, 0)
+        for d in range(24):
+            double(d, 0)
 
     low = lane_low((32, 128))
-    for b in range(GROUP):
+    def back_y(b):
         s0, s1 = slots_of(at, domains[step * GROUP + b])
         weighted = []
         for par in range(2):
@@ -222,7 +246,8 @@
             level = jnp.concatenate([level, level], axis=0)
             weighted.append(level * fine[b, par])
         col[b] = weighted[0].astype(F32) + jnp.dot(weighted[1], wide_t[...], preferred_element_type=F32)
-    for b in range(GROUP):
+
+    def back_x(b):
         for i in range(2):
             odd = col[b, 128 * i + 64 : 128 * i + 128].astype(BF16)
             res = col[b, 128 * i : 128 * i + 64] + jnp.dot(odd_xt[...], odd, preferred_element_type=F32)
@@ -232,16 +257,18 @@
                 f = 4 * i + 2 * k
                 stage[b, pl.ds(f, 32, stride=8), :] = jnp.where(low, p0, pltpu.roll(p1, 64, 1))
                 stage[b, pl.ds(f + 1, 32, stride=8), :] = jnp.where(low, pltpu.roll(p0, 64, 1), p1)
-    for b in range(GROUP):
-        for c in range(32):
-            out[b, :, 128 * c : 128 * c + 128] = stage[b, 8 * c : 8 * c + 8, :].astype(BF16)
+
+    def regroup(b):
+        out[b] = stage[b].astype(BF16)
+
+    in_turn((back_y, back_x, regroup), GROUP)
 
 
 def box_apply(at, domains, pot, fine):
     boxes = fine.shape[0]
     odd_x, wide = tables()
     steps = boxes // GROUP
-    return pl.pallas_call(
+    out = pl.pallas_call(
         apply_kernel,
         grid_spec=pltpu.PrefetchScalarGridSpec(
             num_scalar_prefetch=2,
@@ -252,18 +279,19 @@
                 pl.BlockSpec((64, 64), lambda i, *_: (0, 0)),
                 pl.BlockSpec((256, 256), lambda i, *_: (0, 0)),
             ],
-            out_specs=pl.BlockSpec((GROUP, 8, 4096), lambda i, *_: (i, 0, 0)),
+            out_specs=pl.BlockSpec((GROUP, 256, 128), lambda i, *_: (i, 0, 0)),
             scratch_shapes=[
                 pltpu.VMEM((24, 2, 64, 128), BF16),
                 pltpu.VMEM((GROUP, 256, 128), F32),
                 pltpu.VMEM((GROUP, 256, 256), F32),
             ],
         ),
-        out_shape=jax.ShapeDtypeStruct((boxes, 8, 4096), BF16),
-        compiler_params=pltpu.CompilerParams(vmem_limit_bytes=VMEM_LIMIT),
+        out_shape=jax.ShapeDtypeStruct((boxes, 256, 128), BF16),
+        compiler_params=pltpu.CompilerParams(vmem_limit_bytes=60 * 1024 * 1024),
         cost_estimate=pl.CostEstimate(flops=10**9, bytes_accessed=27 * 10**6, transcendentals=0),
         name="box_apply",
     )(at, domains, pot, fine, jnp.asarray(np.ascontiguousarray(odd_x.T)), jnp.asarray(np.ascontiguousarray(wide.T)))
+    return out.reshape(boxes, 32, 8, 128).transpose(0, 2, 1, 3).reshape(boxes, 8, 4096)
 
 
 def permuted(rows, cols, a, back):
@@ -283,16 +311,26 @@
     out[...] = permuted(rows, cols, pot[at_x[0]].astype(F32), True).astype(BF16)
 
 
+def potential_kernel(at_x, *refs):
+    got, pot = refs[:4], refs[4]
+    for s in range(4):
+        x = lax.rem(at_x[0] - s + 4, 4)
+        total = sum(g[x].astype(F32) for g in got)
+        kernel = got[s][4].astype(F32) + got[s][5].astype(F32)
+        pot[x] = (total * kernel).astype(BF16)
+
+
 def small_call(kernel, scalars, arrays, shape, name):
     smem, vmem = pl.BlockSpec(memory_space=pltpu.SMEM), pl.BlockSpec(memory_space=pltpu.VMEM)
     return pl.pallas_call(
         kernel,
-        in_specs=[smem] * len(scalars) + [vmem] * (len(arrays) + 2),
+        in_specs=[smem] * len(scalars) + [vmem] * len(arrays),
         out_specs=vmem,
         out_shape=jax.ShapeDtypeStruct(shape, BF16),
         cost_estimate=pl.CostEstimate(flops=10**7, bytes_accessed=10**6, transcendentals=0),
+        compiler_params=pltpu.CompilerParams(vmem_limit_bytes=4 * 1024 * 1024),
         name=name,
-    )(*scalars, *arrays, *(jnp.asarray(o) for o in cell_orders()))
+    )(*scalars, *arrays)
 
 
 def shifted(array, axis, by):
@@ -304,25 +342,19 @@
     at_x, at_y, at_z = (lax.axis_index(a) for a in AXES)
     at = jnp.stack([at_y, at_z])
     domains = box_domain.reshape(-1)
-    part, fine = box_density(at, domains, functions, responses, pair_index, pair_weight)
-    kxc = small_call(store_kernel, (), (kernel_xc.reshape(64, 128),), (2, 64, 128), "kernel_order")
-
-    part = part.reshape(3, 2, 4, 64, 128)
-    lower = shifted(part[0], "gz", -1)
-    upper = shifted(part[2], "gz", 1)
-    by_z = (part[1].astype(F32) + lower.astype(F32) + upper.astype(F32)).astype(BF16)
-    by_y = (by_z[1].astype(F32) + shifted(by_z[0], "gy", -1).astype(F32)).astype(BF16)
+    *parts, fine = box_density(at, domains, functions, responses, pair_index, pair_weight)
+    orders = [jnp.asarray(o) for o in cell_orders()]
+    kxc = small_call(store_kernel, (), (kernel_xc.reshape(64, 128), *orders), (2, 64, 128), "kernel_order")
+
+    lower = shifted(parts[0], "gz", -1)
+    upper = shifted(parts[2], "gz", 1)
+    by_z = (parts[1].astype(F32) + lower.astype(F32) + upper.astype(F32)).astype(BF16)
+    by_y = (by_z[4:].astype(F32) + shifted(by_z[:4], "gy", -1).astype(F32)).astype(BF16)
     sent = jnp.concatenate([by_y, kxc])
     got = [sent] + [shifted(sent, "gx", s) for s in (1, 2, 3)]
-    total = sum(g[:4].astype(F32) for g in got)
-    pot = []
-    for x in range(4):
-        which = (at_x - x) % 4
-        high, low = (lax.select_n(which, *(g[k] for g in got)).astype(F32) for k in (4, 5))
-        pot.append((total[x] * (high + low)).astype(BF16))
-    pot = jnp.stack(pot)
+    pot = small_call(potential_kernel, (at_x.reshape(1),), got, (4, 64, 128), "potential")
     by_y = jnp.stack([shifted(pot, "gy", 1), pot])
-    natural = small_call(natural_kernel, (at_x.reshape(1),), (pot,), (64, 128), "natural_order")
+    natural = small_call(natural_kernel, (at_x.reshape(1),), (pot, *orders), (64, 128), "natural_order")
     by_z = jnp.stack([shifted(by_y, "gz", 1), by_y, shifted(by_y, "gz", -1)]).reshape(24, 64, 128)
     applied = box_apply(at, domains, by_z, fine)
     return applied, natural.reshape(1, 8192)

time: 86.9 us -> 75.7 us (0.87)
  Pallas kernels: 47.3 us -> 37.1 us
  waiting for transfers between devices: 16.5 us -> 21.8 us
  other arithmetic: 5.4 us -> 2.46 us
  local copies, waits for them, and re-layouts: 2.42 us -> 0.67 us
    ppermute x9, waiting for transfers between devices: 16.5 us -> 21.8 us  [shifted(): lax.ppermute(array, axis, [(i, (i + by) % size) for i in range(size)])]
    pallas_call x1, Pallas kernels: 18 us -> 14.1 us  [box_apply(): pl.pallas_call(apply_kernel, grid_spec=pltpu.PrefetchScalarGridSpec(num_s...]
    pallas_call x1, Pallas kernels: 25.4 us -> 22.1 us  [box_density(): pl.pallas_call(density_kernel, grid_spec=pltpu.PrefetchScalarGridSpec(num...]
    pallas_call x2 -> x3, Pallas kernels: 3.82 us -> 0.82 us  [small_call(): pl.pallas_call(kernel, in_specs=[smem] * len(scalars) + [vmem] * len(arra...]
    convert_element_type x6 -> x2, other arithmetic: 3.11 us -> 0.98 us  [the longest x1 0.96 us: on_device(): (parts[1].astype(F32) + lower.astype(F32) + upper.astype(F32)).astype(BF16)]
    slice x1, local copies, waits for them, and re-layouts: 1.06 us -> 0.01 us  [on_device(): by_z[:4]]
  transfers between devices with their start and end apart: 9 -> 9, of which waited for: 6 -> 9; matrix products, arithmetic and copies ran while one was open for 2% -> 1% of each run, Pallas kernels for 4% -> 1%
where the time goes in v2:
time: 75.7 us; the launch traced here: 75.4 us
  Pallas kernels  37.1 us (49%)
  waiting for transfers between devices  21.8 us (29%)
  starting transfers between devices  12.7 us (17%)
  other arithmetic  2.46 us (3%)
    pallas_call x1, Pallas kernels, box_density(): pl.pallas_call(density_kernel, grid_spec=pltpu.PrefetchScalarGridSpec(num...  22.1 us
    ppermute x9, waiting for transfers between devices, shifted(): lax.ppermute(array, axis, [(i, (i + by) % size) for i in range(size)])  21.8 us
    pallas_call x1, Pallas kernels, box_apply(): pl.pallas_call(apply_kernel, grid_spec=pltpu.PrefetchScalarGridSpec(num_s...  14.1 us
    ppermute x9, starting transfers between devices, shifted(): lax.ppermute(array, axis, [(i, (i + by) % size) for i in range(size)])  12.7 us
  transfers between devices with their start and end apart: 9, of which 9 were waited for; matrix products, arithmetic and copies ran while one was open for 1% of the time, Pallas kernels for 1%

profile of v2, /device:TPU:0, one launch (start us, length us, event | category | flops | bytes accessed | tf_op | source)
XLA Modules:
  0.0 75.4 jit_solution(3483469472856113641)
XLA Ops:
  0.6 0.6 pad_add_fusion.at
  1.3 0.0 copy-start
  1.3 0.0 copy-start.1
  1.3 0.0 copy-start.2
  1.3 22.1 %box_density.1 = (bf16[8,64,128]{2,1,0:T(8,128)(2,1)}, bf16[8,64,128]{2,1,0:T(8,128)(2,1)}, bf16[8,64,128]{2,1,0:T(8,128)(2,1)}, bf16[80,2,256,256]{3,2,1,0:T(8,128)(2,1)}) custom-call(s32[2]{0:T(128)} %pad_add_fusion.at, s32[80]{0:T(128)} %bitcast.47, bf16[80,256,128]{2,1,0:T(8,128)(2,1)} %bitcast.37, bf16[80,256,128]{2,1,0:T(8,128)(2,1)} %bitcast.38, ...), custom_call_target="tpu_custom_call" | custom-call | flops 2000000000 | bytes 32000000 | tf_op jit(solution)/shard_map/box_density/pallas_call | solution.py:173
  23.4 3.6 %collective-permute-start = (bf16[8,64,128]{2,1,0:T(8,128)(2,1)}, bf16[8,64,128]{2,1,0:T(8,128)(2,1)S(1)}, u32[]{:S(2)}, u32[]{:S(2)}) collective-permute-start(bf16[8,64,128]{2,1,0:T(8,128)(2,1)} %get-tuple-element.7), channel_id=1, source_target_pairs={{0,7},{1,0},{2,1},{3,2},{4,3},{5,4},{6,5},{7,6},{8,15},{9,8},{10,9... | collective-permute-start | bytes 393224 | tf_op jit(solution)/shard_map/ppermute | solution.py:338
  27.0 0.0 collective-permute-start.1
  27.0 2.8 %collective-permute-done = bf16[8,64,128]{2,1,0:T(8,128)(2,1)S(1)} collective-permute-done((bf16[8,64,128]{2,1,0:T(8,128)(2,1)}, bf16[8,64,128]{2,1,0:T(8,128)(2,1)S(1)}, u32[]{:S(2)}, u32[]{:S(2)}) %collective-permute-start) | collective-permute-done | bytes 131104 | tf_op jit(solution)/shard_map/ppermute | solution.py:338
  29.8 3.0 %collective-permute-done.1 = bf16[8,64,128]{2,1,0:T(8,128)(2,1)S(1)} collective-permute-done((bf16[8,64,128]{2,1,0:T(8,128)(2,1)}, bf16[8,64,128]{2,1,0:T(8,128)(2,1)S(1)}, u32[]{:S(2)}, u32[]{:S(2)}) %collective-permute-start.1) | collective-permute-done | bytes 131104 | tf_op jit(solution)/shard_map/ppermute | solution.py:338
  32.8 1.0 %add_convert_fusion = bf16[8,64,128]{2,1,0:T(8,128)(2,1)S(1)} fusion(bf16[8,64,128]{2,1,0:T(8,128)(2,1)S(1)} %collective-permute-done.1, bf16[8,64,128]{2,1,0:T(8,128)(2,1)S(1)} %collective-permute-done, bf16[8,64,128]{2,1,0:T(8,128)(2,1)} %get-tuple-element.6), kind=kLoop, calls=%fused_computation.1 | loop fusion | flops 393216 | bytes 524288 | tf_op jit(solution)/shard_map/convert_element_type | solution.py:351
  33.8 3.1 %collective-permute-start.2 = (bf16[4,64,128]{2,1,0:T(8,128)(2,1)S(1)}, bf16[4,64,128]{2,1,0:T(8,128)(2,1)S(1)}, u32[]{:S(2)}, u32[]{:S(2)}) collective-permute-start(bf16[4,64,128]{2,1,0:T(8,128)(2,1)S(1)} %slice.9), channel_id=1, source_target_pairs={{0,24},{8,0},{16,8},{24,16},{1,25},{9,1},{17,9},{25,17},{2,26},{10... | collective-permute-start | bytes 196616 | tf_op jit(solution)/shard_map/ppermute | solution.py:338
  36.9 0.0 copy-done
  36.9 0.0 copy-done.1
  36.9 0.0 copy-done.2
  36.9 0.4 kernel_order.1
  37.3 1.5 %collective-permute-done.2 = bf16[4,64,128]{2,1,0:T(8,128)(2,1)S(1)} collective-permute-done((bf16[4,64,128]{2,1,0:T(8,128)(2,1)S(1)}, bf16[4,64,128]{2,1,0:T(8,128)(2,1)S(1)}, u32[]{:S(2)}, u32[]{:S(2)}) %collective-permute-start.2) | collective-permute-done | bytes 65568 | tf_op jit(solution)/shard_map/ppermute | solution.py:338
  38.8 2.8 %collective-permute-start.5 = (bf16[6,64,128]{2,1,0:T(8,128)(2,1)S(1)}, bf16[6,64,128]{2,1,0:T(8,128)(2,1)S(1)}, u32[]{:S(2)}, u32[]{:S(2)}) collective-permute-start(bf16[6,64,128]{2,1,0:T(8,128)(2,1)S(1)} %pad_maximum_fusion.2.refs_0_), channel_id=1, source_target_pairs={{0,96},{32,0},{64,32},{96,64},{1,97},{33,1},{65,33},{97,65},{2,98}... | collective-permute-start | bytes 294920 | tf_op jit(solution)/shard_map/ppermute | solution.py:338
  41.6 0.8 %collective-permute-start.4 = (bf16[6,64,128]{2,1,0:T(8,128)(2,1)S(1)}, bf16[6,64,128]{2,1,0:T(8,128)(2,1)S(1)}, u32[]{:S(2)}, u32[]{:S(2)}) collective-permute-start(bf16[6,64,128]{2,1,0:T(8,128)(2,1)S(1)} %pad_maximum_fusion.2.refs_0_), channel_id=1, source_target_pairs={{0,64},{32,96},{64,0},{96,32},{1,65},{33,97},{65,1},{97,33},{2,66}... | collective-permute-start | bytes 294920 | tf_op jit(solution)/shard_map/ppermute | solution.py:338
  42.5 0.9 %collective-permute-start.3 = (bf16[6,64,128]{2,1,0:T(8,128)(2,1)S(1)}, bf16[6,64,128]{2,1,0:T(8,128)(2,1)S(1)}, u32[]{:S(2)}, u32[]{:S(2)}) collective-permute-start(bf16[6,64,128]{2,1,0:T(8,128)(2,1)S(1)} %pad_maximum_fusion.2.refs_0_), channel_id=1, source_target_pairs={{0,32},{32,64},{64,96},{96,0},{1,33},{33,65},{65,97},{97,1},{2,34}... | collective-permute-start | bytes 294920 | tf_op jit(solution)/shard_map/ppermute | solution.py:338
  43.3 0.5 collective-permute-done.5.refs_3_
  43.9 4.0 %collective-permute-done.4.refs_2_ = bf16[6,64,128]{2,1,0:T(8,128)(2,1)S(1)} collective-permute-done((bf16[6,64,128]{2,1,0:T(8,128)(2,1)S(1)}, bf16[6,64,128]{2,1,0:T(8,128)(2,1)S(1)}, u32[]{:S(2)}, u32[]{:S(2)}) %collective-permute-start.4) | collective-permute-done | bytes 98336 | tf_op jit(solution)/shard_map/ppermute | solution.py:338
  47.8 1.0 %collective-permute-done.3.refs_1_ = bf16[6,64,128]{2,1,0:T(8,128)(2,1)S(1)} collective-permute-done((bf16[6,64,128]{2,1,0:T(8,128)(2,1)S(1)}, bf16[6,64,128]{2,1,0:T(8,128)(2,1)S(1)}, u32[]{:S(2)}, u32[]{:S(2)}) %collective-permute-start.3) | collective-permute-done | bytes 98336 | tf_op jit(solution)/shard_map/ppermute | solution.py:338
  48.8 0.1 potential.1.pot
  48.9 1.0 %collective-permute-start.6 = (bf16[4,64,128]{2,1,0:T(8,128)(2,1)S(1)}, bf16[4,64,128]{2,1,0:T(8,128)(2,1)S(1)}, u32[]{:S(2)}, u32[]{:S(2)}) collective-permute-start(bf16[4,64,128]{2,1,0:T(8,128)(2,1)S(1)} %potential.1.pot), channel_id=1, source_target_pairs={{0,8},{8,16},{16,24},{24,0},{1,9},{9,17},{17,25},{25,1},{2,10},{10... | collective-permute-start | bytes 196616 | tf_op jit(solution)/shard_map/ppermute | solution.py:338
  49.9 4.9 %collective-permute-done.6 = bf16[4,64,128]{2,1,0:T(8,128)(2,1)S(1)} collective-permute-done((bf16[4,64,128]{2,1,0:T(8,128)(2,1)S(1)}, bf16[4,64,128]{2,1,0:T(8,128)(2,1)S(1)}, u32[]{:S(2)}, u32[]{:S(2)}) %collective-permute-start.6) | collective-permute-done | bytes 65568 | tf_op jit(solution)/shard_map/ppermute | solution.py:338
  54.8 0.0 collective-permute-start.8
  54.8 0.5 collective-permute-start.7
  55.3 0.3 natural_order.1
  55.7 0.7 copy.17
  56.3 1.0 %collective-permute-done.8 = bf16[2,4,64,128]{3,2,1,0:T(8,128)(2,1)S(1)} collective-permute-done((bf16[2,4,64,128]{3,2,1,0:T(8,128)(2,1)S(1)}, bf16[2,4,64,128]{3,2,1,0:T(8,128)(2,1)S(1)}, u32[]{:S(2)}, u32[]{:S(2)}) %collective-permute-start.8) | collective-permute-done | bytes 131104 | tf_op jit(solution)/shard_map/ppermute | solution.py:338
  57.3 3.1 %collective-permute-done.7 = bf16[2,4,64,128]{3,2,1,0:T(8,128)(2,1)S(1)} collective-permute-done((bf16[2,4,64,128]{3,2,1,0:T(8,128)(2,1)S(1)}, bf16[2,4,64,128]{3,2,1,0:T(8,128)(2,1)S(1)}, u32[]{:S(2)}, u32[]{:S(2)}) %collective-permute-start.7) | collective-permute-done | bytes 131104 | tf_op jit(solution)/shard_map/ppermute | solution.py:338
  60.4 0.8 %pad_maximum_fusion = bf16[3,2,4,64,128]{4,3,2,1,0:T(8,128)(2,1)} fusion(bf16[1,2,4,64,128]{4,3,2,1,0:T(8,128)(2,1)S(1)} %bitcast.41, bf16[1,2,4,64,128]{4,3,2,1,0:T(8,128)(2,1)S(1)} %get-tuple-element.10, bf16[1,2,4,64,128]{4,3,2,1,0:T(8,128)(2,1)S(1)} %bitcast.42), kind=kLoop, calls=%fused_computation | loop fusion | flops 393216 | bytes 786432 | tf_op jit(solution)/shard_map/stack | solution.py:358
  61.2 14.1 %box_apply.1 = bf16[80,256,128]{2,1,0:T(8,128)(2,1)} custom-call(s32[2]{0:T(128)} %pad_add_fusion.at, s32[80]{0:T(128)} %bitcast.48, bf16[24,64,128]{2,1,0:T(8,128)(2,1)} %bitcast.40, bf16[80,2,256,256]{3,2,1,0:T(8,128)(2,1)} %get-tuple-element.9.fine, bf16[64,64]{1,0:T(8,128)(2,1)} %constant.31.clone.odd_xt, bf16[256,256]{1,0:T(8,128)(2,1)} %constant.32.clone.wide_t), custom_call_target="tpu_custom_call" | custom-call | flops 1000000000 | bytes 27000000 | tf_op jit(solution)/shard_map/box_apply/pallas_call | solution.py:271
  (4 shorter events, 0.1 us)
Async XLA Ops:
  1.3 35.6 %copy-start = (f32[128,128]{1,0:T(8,128)S(1)}, f32[128,128]{1,0:T(8,128)}, u32[]{:S(2)}) copy-start(f32[128,128]{1,0:T(8,128)} %constant.30.clone.cols) | copy-start | bytes 196612
  1.3 35.6 %copy-start.1 = (f32[64,64]{1,0:T(8,128)S(1)}, f32[64,64]{1,0:T(8,128)}, u32[]{:S(2)}) copy-start(f32[64,64]{1,0:T(8,128)} %constant.29.clone.rows) | copy-start | bytes 49156
  1.3 35.6 %copy-start.2 = (f32[1,8192]{1,0:T(1,128)S(1)}, f32[1,8192]{1,0:T(1,128)}, u32[]{:S(2)}) copy-start(f32[1,8192]{1,0:T(1,128)} %param.18) | copy-start | bytes 98308
  23.4 6.4 %collective-permute-start = (bf16[8,64,128]{2,1,0:T(8,128)(2,1)}, bf16[8,64,128]{2,1,0:T(8,128)(2,1)S(1)}, u32[]{:S(2)}, u32[]{:S(2)}) collective-permute-start(bf16[8,64,128]{2,1,0:T(8,128)(2,1)} %get-tuple-element.7), channel_id=1, source_target_pairs={{0,7},{1,0},{2,1},{3,2},{4,3},{5,4},{6,5},{7,6},{8,15},{9,8},{10,9... | collective-permute-start | bytes 393224 | tf_op jit(solution)/shard_map/ppermute | solution.py:338
  27.0 5.8 %collective-permute-start.1 = (bf16[8,64,128]{2,1,0:T(8,128)(2,1)}, bf16[8,64,128]{2,1,0:T(8,128)(2,1)S(1)}, u32[]{:S(2)}, u32[]{:S(2)}) collective-permute-start(bf16[8,64,128]{2,1,0:T(8,128)(2,1)} %get-tuple-element.8), channel_id=1, source_target_pairs={{0,1},{1,2},{2,3},{3,4},{4,5},{5,6},{6,7},{7,0},{8,9},{9,10},{10,1... | collective-permute-start | bytes 393224 | tf_op jit(solution)/shard_map/ppermute | solution.py:338
  33.8 5.0 %collective-permute-start.2 = (bf16[4,64,128]{2,1,0:T(8,128)(2,1)S(1)}, bf16[4,64,128]{2,1,0:T(8,128)(2,1)S(1)}, u32[]{:S(2)}, u32[]{:S(2)}) collective-permute-start(bf16[4,64,128]{2,1,0:T(8,128)(2,1)S(1)} %slice.9), channel_id=1, source_target_pairs={{0,24},{8,0},{16,8},{24,16},{1,25},{9,1},{17,9},{25,17},{2,26},{10... | collective-permute-start | bytes 196616 | tf_op jit(solution)/shard_map/ppermute | solution.py:338
  38.8 5.0 %collective-permute-start.5 = (bf16[6,64,128]{2,1,0:T(8,128)(2,1)S(1)}, bf16[6,64,128]{2,1,0:T(8,128)(2,1)S(1)}, u32[]{:S(2)}, u32[]{:S(2)}) collective-permute-start(bf16[6,64,128]{2,1,0:T(8,128)(2,1)S(1)} %pad_maximum_fusion.2.refs_0_), channel_id=1, source_target_pairs={{0,96},{32,0},{64,32},{96,64},{1,97},{33,1},{65,33},{97,65},{2,98}... | collective-permute-start | bytes 294920 | tf_op jit(solution)/shard_map/ppermute | solution.py:338
  41.6 6.2 %collective-permute-start.4 = (bf16[6,64,128]{2,1,0:T(8,128)(2,1)S(1)}, bf16[6,64,128]{2,1,0:T(8,128)(2,1)S(1)}, u32[]{:S(2)}, u32[]{:S(2)}) collective-permute-start(bf16[6,64,128]{2,1,0:T(8,128)(2,1)S(1)} %pad_maximum_fusion.2.refs_0_), channel_id=1, source_target_pairs={{0,64},{32,96},{64,0},{96,32},{1,65},{33,97},{65,1},{97,33},{2,66}... | collective-permute-start | bytes 294920 | tf_op jit(solution)/shard_map/ppermute | solution.py:338
  42.5 6.4 %collective-permute-start.3 = (bf16[6,64,128]{2,1,0:T(8,128)(2,1)S(1)}, bf16[6,64,128]{2,1,0:T(8,128)(2,1)S(1)}, u32[]{:S(2)}, u32[]{:S(2)}) collective-permute-start(bf16[6,64,128]{2,1,0:T(8,128)(2,1)S(1)} %pad_maximum_fusion.2.refs_0_), channel_id=1, source_target_pairs={{0,32},{32,64},{64,96},{96,0},{1,33},{33,65},{65,97},{97,1},{2,34}... | collective-permute-start | bytes 294920 | tf_op jit(solution)/shard_map/ppermute | solution.py:338
  48.9 5.9 %collective-permute-start.6 = (bf16[4,64,128]{2,1,0:T(8,128)(2,1)S(1)}, bf16[4,64,128]{2,1,0:T(8,128)(2,1)S(1)}, u32[]{:S(2)}, u32[]{:S(2)}) collective-permute-start(bf16[4,64,128]{2,1,0:T(8,128)(2,1)S(1)} %potential.1.pot), channel_id=1, source_target_pairs={{0,8},{8,16},{16,24},{24,0},{1,9},{9,17},{17,25},{25,1},{2,10},{10... | collective-permute-start | bytes 196616 | tf_op jit(solution)/shard_map/ppermute | solution.py:338
  54.8 2.5 %collective-permute-start.8 = (bf16[2,4,64,128]{3,2,1,0:T(8,128)(2,1)S(1)}, bf16[2,4,64,128]{3,2,1,0:T(8,128)(2,1)S(1)}, u32[]{:S(2)}, u32[]{:S(2)}) collective-permute-start(bf16[2,4,64,128]{3,2,1,0:T(8,128)(2,1)S(1)} %get-tuple-element.11), channel_id=1, source_target_pairs={{0,7},{1,0},{2,1},{3,2},{4,3},{5,4},{6,5},{7,6},{8,15},{9,8},{10,9... | collective-permute-start | bytes 393224 | tf_op jit(solution)/shard_map/ppermute | solution.py:338
  54.8 5.6 %collective-permute-start.7 = (bf16[2,4,64,128]{3,2,1,0:T(8,128)(2,1)S(1)}, bf16[2,4,64,128]{3,2,1,0:T(8,128)(2,1)S(1)}, u32[]{:S(2)}, u32[]{:S(2)}) collective-permute-start(bf16[2,4,64,128]{3,2,1,0:T(8,128)(2,1)S(1)} %get-tuple-element.11), channel_id=1, source_target_pairs={{0,1},{1,2},{2,3},{3,4},{4,5},{5,6},{6,7},{7,0},{8,9},{9,10},{10,1... | collective-permute-start | bytes 393224 | tf_op jit(solution)/shard_map/ppermute | solution.py:338

commit v3 on v2

--- a/solution.py
+++ b/solution.py
@@ -9,7 +9,8 @@
 
 AXES = ("gx", "gy", "gz")
 GROUP = 16
-LAG = 1
+HELD = 8
+SLOTS = 4
 BF16 = jnp.bfloat16
 F32 = jnp.float32
 
@@ -54,14 +55,14 @@
     return base + box_x, base + lax.rem(box_x + 1, 4)
 
 
-def in_turn(stages, lag=LAG):
-    for t in range(GROUP + lag * (len(stages) - 1)):
+def in_turn(stages, boxes, lag=1):
+    for t in range(boxes + lag * (len(stages) - 1)):
         for i, stage in enumerate(stages):
-            if 0 <= t - lag * i < GROUP:
+            if 0 <= t - lag * i < boxes:
                 stage(t - lag * i)
 
 
-def density_kernel(at, domains, func, resp, pidx, pw, spread, odd_x, wide, part0, part1, part2, fine, acc, stage, mixer, rs):
+def density_kernel(at_y, at_z, domains, func, resp, pidx, pw, spread, odd_x, wide, part0, part1, part2, fine, acc, stage, mixer, rs):
     step = pl.program_id(0)
     rows8 = 8 * GROUP
 
@@ -132,20 +133,18 @@
     def along_y(b):
         tall_f = fine[b, 0]
         tall_r = rs[b]
-        shift_f = jnp.dot(tall_f, wide[...], preferred_element_type=F32)
-        shift_r = jnp.dot(tall_r, wide[...], preferred_element_type=F32)
-        fine[b, 1] = shift_f.astype(BF16)
-        den_e = tall_f.astype(F32) * tall_r.astype(F32)
-        den_o = shift_f * shift_r
-        s0, s1 = slots_of(at, domains[step * GROUP + b])
-        for par, den in ((0, den_e), (1, den_o)):
+        shift_f = jnp.dot(tall_f, wide[...], preferred_element_type=F32).astype(BF16)
+        shift_r = jnp.dot(tall_r, wide[...], preferred_element_type=F32).astype(BF16)
+        fine[b, 1] = shift_f
+        s0, s1 = slots_of((at_y[0], at_z[0]), domains[step * GROUP + b])
+        for par, den in ((0, tall_f * tall_r), (1, shift_f * shift_r)):
             den = den[:128] + den[128:]
-            den = den[:, :128] + den[:, 128:]
+            den = (den[:, :128] + den[:, 128:]).astype(F32)
             for g in range(4):
                 acc[s0, par, 16 * g : 16 * g + 16] += den[32 * g : 32 * g + 16]
                 acc[s1, par, 16 * g : 16 * g + 16] += den[32 * g + 16 : 32 * g + 32]
 
-    in_turn((mix, regroup, along_x, along_y))
+    in_turn((mix, regroup, along_x, along_y), GROUP)
 
     @pl.when(step == pl.num_programs(0) - 1)
     def _():
@@ -170,10 +169,19 @@
     odd_x, wide = tables()
     steps = boxes // GROUP
     spread = np.repeat(np.eye(boxes, dtype=np.float32), 8, axis=1)
+    arrays = (
+        as_tiles(functions),
+        as_tiles(responses),
+        jnp.transpose(pair_index, (0, 2, 1)),
+        jnp.transpose(pair_weight, (1, 0)),
+        jnp.asarray(spread),
+        jnp.asarray(odd_x),
+        jnp.asarray(wide),
+    )
     return pl.pallas_call(
         density_kernel,
         grid_spec=pltpu.PrefetchScalarGridSpec(
-            num_scalar_prefetch=2,
+            num_scalar_prefetch=3,
             grid=(steps,),
             in_specs=[
                 pl.BlockSpec((GROUP, 256, 128), lambda i, *_: (i, 0, 0)),
@@ -199,31 +207,40 @@
             *[jax.ShapeDtypeStruct((8, 64, 128), BF16)] * 3,
             jax.ShapeDtypeStruct((boxes, 2, 256, 256), BF16),
         ],
-        compiler_params=pltpu.CompilerParams(vmem_limit_bytes=60 * 1024 * 1024),
+        compiler_params=pltpu.CompilerParams(vmem_limit_bytes=44 * 1024 * 1024),
         cost_estimate=pl.CostEstimate(flops=2 * 10**9, bytes_accessed=32 * 10**6, transcendentals=0),
         name="box_density",
     )(
-        at,
+        *at,
         domains,
-        as_tiles(functions),
-        as_tiles(responses),
-        jnp.transpose(pair_index, (0, 2, 1)),
-        jnp.transpose(pair_weight, (1, 0)),
-        jnp.asarray(spread),
-        jnp.asarray(odd_x),
-        jnp.asarray(wide),
+        *(pltpu.with_memory_space_constraint(array, pltpu.HBM) for array in arrays),
     )
 
 
-def apply_kernel(at, domains, pot, fine, odd_xt, wide_t, out, twice, stage, col):
+def apply_kernel(at_y, at_z, domains, pot0, pot1, pot2, fine, odd_xt, wide_t, out, twice, stage, col, held, sems):
     step = pl.program_id(0)
+    steps = pl.num_programs(0) - 1
+
+    def fetch(i):
+        slot = lax.rem(i, SLOTS)
+        return pltpu.make_async_copy(fine.at[pl.ds(i * HELD, HELD)], held.at[slot], sems.at[slot])
 
     @pl.when(step == 0)
     def _():
+        for i in range(SLOTS - 1):
+            fetch(i).start()
+
+    @pl.when(step + SLOTS - 1 < steps)
+    def _():
+        fetch(step + SLOTS - 1).start()
+
+
+    @pl.when(step == 0)
+    def _():
         lowd = lane_low((64, 128))
 
         def double(d, _):
-            own = pot[d].astype(F32) * 0.25
+            own = (pot0, pot1, pot2)[d // 8][d % 8].astype(F32) * 0.25
             other = pltpu.roll(own, 64, 1)
             twice[d, 0] = jnp.where(lowd, own, other).astype(BF16)
             twice[d, 1] = jnp.where(lowd, other, own).astype(BF16)
@@ -232,9 +249,16 @@
         for d in range(24):
             double(d, 0)
 
+    @pl.when(step < steps)
+    def _():
+        fetch(step).wait()
+
     low = lane_low((32, 128))
+    now = lax.rem(step, SLOTS)
+    ahead = jnp.minimum(step, steps - 1) * HELD
+
     def back_y(b):
-        s0, s1 = slots_of(at, domains[step * GROUP + b])
+        s0, s1 = slots_of((at_y[0], at_z[0]), domains[ahead + b])
         weighted = []
         for par in range(2):
             pieces = []
@@ -244,7 +268,7 @@
             level = jnp.concatenate(pieces, axis=0)
             level = jnp.concatenate([level, level], axis=1)
             level = jnp.concatenate([level, level], axis=0)
-            weighted.append(level * fine[b, par])
+            weighted.append(level * held[now, b, par])
         col[b] = weighted[0].astype(F32) + jnp.dot(weighted[1], wide_t[...], preferred_element_type=F32)
 
     def back_x(b):
@@ -261,36 +285,39 @@
     def regroup(b):
         out[b] = stage[b].astype(BF16)
 
-    in_turn((back_y, back_x, regroup), GROUP)
-
-
-def box_apply(at, domains, pot, fine):
+    in_turn((back_x, regroup, back_y), HELD)
+
+
+def box_apply(at, domains, pots, fine):
     boxes = fine.shape[0]
+    fine = pltpu.with_memory_space_constraint(fine, pltpu.HBM)
     odd_x, wide = tables()
-    steps = boxes // GROUP
+    steps = boxes // HELD
     out = pl.pallas_call(
         apply_kernel,
         grid_spec=pltpu.PrefetchScalarGridSpec(
-            num_scalar_prefetch=2,
-            grid=(steps,),
+            num_scalar_prefetch=3,
+            grid=(steps + 1,),
             in_specs=[
-                pl.BlockSpec((24, 64, 128), lambda i, *_: (0, 0, 0)),
-                pl.BlockSpec((GROUP, 2, 256, 256), lambda i, *_: (i, 0, 0, 0)),
+                *[pl.BlockSpec((8, 64, 128), lambda i, *_: (0, 0, 0))] * 3,
+                pl.BlockSpec(memory_space=pl.ANY),
                 pl.BlockSpec((64, 64), lambda i, *_: (0, 0)),
                 pl.BlockSpec((256, 256), lambda i, *_: (0, 0)),
             ],
-            out_specs=pl.BlockSpec((GROUP, 256, 128), lambda i, *_: (i, 0, 0)),
+            out_specs=pl.BlockSpec((HELD, 256, 128), lambda i, *_: (jnp.maximum(i - 1, 0), 0, 0)),
             scratch_shapes=[
                 pltpu.VMEM((24, 2, 64, 128), BF16),
-                pltpu.VMEM((GROUP, 256, 128), F32),
-                pltpu.VMEM((GROUP, 256, 256), F32),
+                pltpu.VMEM((HELD, 256, 128), F32),
+                pltpu.VMEM((HELD, 256, 256), F32),
+                pltpu.VMEM((SLOTS, HELD, 2, 256, 256), BF16),
+                pltpu.SemaphoreType.DMA((SLOTS,)),
             ],
         ),
         out_shape=jax.ShapeDtypeStruct((boxes, 256, 128), BF16),
-        compiler_params=pltpu.CompilerParams(vmem_limit_bytes=60 * 1024 * 1024),
+        compiler_params=pltpu.CompilerParams(vmem_limit_bytes=44 * 1024 * 1024),
         cost_estimate=pl.CostEstimate(flops=10**9, bytes_accessed=27 * 10**6, transcendentals=0),
         name="box_apply",
-    )(at, domains, pot, fine, jnp.asarray(np.ascontiguousarray(odd_x.T)), jnp.asarray(np.ascontiguousarray(wide.T)))
+    )(*at, domains, *pots, fine, jnp.asarray(np.ascontiguousarray(odd_x.T)), jnp.asarray(np.ascontiguousarray(wide.T)))
     return out.reshape(boxes, 32, 8, 128).transpose(0, 2, 1, 3).reshape(boxes, 8, 4096)
 
 
@@ -304,7 +331,6 @@
 def store_kernel(kxc, rows, cols, out):
     exact = permuted(rows, cols, kxc[...], False)
     out[0] = exact.astype(BF16)
-    out[1] = (exact - out[0].astype(F32)).astype(BF16)
 
 
 def natural_kernel(at_x, pot, rows, cols, out):
@@ -316,7 +342,7 @@
     for s in range(4):
         x = lax.rem(at_x[0] - s + 4, 4)
         total = sum(g[x].astype(F32) for g in got)
-        kernel = got[s][4].astype(F32) + got[s][5].astype(F32)
+        kernel = got[s][4].astype(F32)
         pot[x] = (total * kernel).astype(BF16)
 
 
@@ -340,11 +366,11 @@
 
 def on_device(functions, responses, box_domain, pair_index, pair_weight, kernel_xc):
     at_x, at_y, at_z = (lax.axis_index(a) for a in AXES)
-    at = jnp.stack([at_y, at_z])
-    domains = box_domain.reshape(-1)
+    at = (at_y.reshape(1), at_z.reshape(1))
+    domains = pltpu.with_memory_space_constraint(box_domain.reshape(-1), pltpu.HBM)
     *parts, fine = box_density(at, domains, functions, responses, pair_index, pair_weight)
     orders = [jnp.asarray(o) for o in cell_orders()]
-    kxc = small_call(store_kernel, (), (kernel_xc.reshape(64, 128), *orders), (2, 64, 128), "kernel_order")
+    kxc = small_call(store_kernel, (), (kernel_xc.reshape(64, 128), *orders), (1, 64, 128), "kernel_order")
 
     lower = shifted(parts[0], "gz", -1)
     upper = shifted(parts[2], "gz", 1)
@@ -353,9 +379,9 @@
     sent = jnp.concatenate([by_y, kxc])
     got = [sent] + [shifted(sent, "gx", s) for s in (1, 2, 3)]
     pot = small_call(potential_kernel, (at_x.reshape(1),), got, (4, 64, 128), "potential")
-    by_y = jnp.stack([shifted(pot, "gy", 1), pot])
+    by_y = jnp.concatenate([shifted(pot, "gy", 1), pot])
     natural = small_call(natural_kernel, (at_x.reshape(1),), (pot, *orders), (64, 128), "natural_order")
-    by_z = jnp.stack([shifted(by_y, "gz", 1), by_y, shifted(by_y, "gz", -1)]).reshape(24, 64, 128)
+    by_z = (shifted(by_y, "gz", 1), by_y, shifted(by_y, "gz", -1))
     applied = box_apply(at, domains, by_z, fine)
     return applied, natural.reshape(1, 8192)
 

time: 75.7 us -> 70.1 us (0.926)
  Pallas kernels: 37.1 us -> 34.4 us
  other arithmetic: 2.46 us -> 0.1 us
    pallas_call x1, Pallas kernels: 14.1 us -> 11.8 us  [box_apply(): pl.pallas_call(apply_kernel, grid_spec=pltpu.PrefetchScalarGridSpec(num_s...]
    another operation x3 -> x0, other arithmetic: 1.47 us -> none  [the longest x2 0.82 us: on_device(): jnp.stack([shifted(by_y, 'gz', 1), by_y, shifted(by_y, 'gz', -1)])]
    convert_element_type x1, other arithmetic: 0.96 us -> 0.06 us  [on_device(): (parts[1].astype(F32) + lower.astype(F32) + upper.astype(F32)).astype(BF16)]
where the time goes in v3:
time: 70.1 us; the launch traced here: 69.9 us
  Pallas kernels  34.4 us (49%)
  waiting for transfers between devices  21.2 us (30%)
  starting transfers between devices  12.7 us (18%)
  between operations  0.73 us (1%)
    pallas_call x1, Pallas kernels, box_density(): pl.pallas_call(density_kernel, grid_spec=pltpu.PrefetchScalarGridSpec(num...  21.8 us
    ppermute x9, waiting for transfers between devices, shifted(): lax.ppermute(array, axis, [(i, (i + by) % size) for i in range(size)])  21.2 us
    ppermute x9, starting transfers between devices, shifted(): lax.ppermute(array, axis, [(i, (i + by) % size) for i in range(size)])  12.7 us
    pallas_call x1, Pallas kernels, box_apply(): pl.pallas_call(apply_kernel, grid_spec=pltpu.PrefetchScalarGridSpec(num_s...  11.8 us
  transfers between devices with their start and end apart: 9, of which 9 were waited for; matrix products, arithmetic and copies ran while one was open for 1% of the time, Pallas kernels for 1%

profile of v3, /device:TPU:0, one launch (start us, length us, event | category | flops | bytes accessed | tf_op | source)
XLA Modules:
  0.0 69.9 jit_solution(4057446473648601158)
XLA Ops:
  0.6 0.0 copy-start
  0.6 0.0 copy-start.2
  0.7 0.0 copy-start.3
  0.7 0.0 copy-start.1
  0.7 0.0 copy-start.4
  0.7 21.8 %box_density.1 = (bf16[8,64,128]{2,1,0:T(8,128)(2,1)S(1)}, bf16[8,64,128]{2,1,0:T(8,128)(2,1)S(1)}, bf16[8,64,128]{2,1,0:T(8,128)(2,1)S(1)}, bf16[80,2,256,256]{3,2,1,0:T(8,128)(2,1)}) custom-call(s32[1]{0:T(128)} %bitcast.at_y, s32[1]{0:T(128)} %bitcast.1.at_z, s32[80]{0:T(128)} %bitcast.35, bf16[80,256,128]{2,1,0:T(8,128)(2,1)} %bitcast.29, ...), custom_call_target="tpu_custom_call" | custom-call | flops 2000000000 | bytes 32000000 | tf_op jit(solution)/shard_map/box_density/pallas_call | solution.py:181
  22.5 3.6 %collective-permute-start = (bf16[8,64,128]{2,1,0:T(8,128)(2,1)S(1)}, bf16[8,64,128]{2,1,0:T(8,128)(2,1)S(1)}, u32[]{:S(2)}, u32[]{:S(2)}) collective-permute-start(bf16[8,64,128]{2,1,0:T(8,128)(2,1)S(1)} %get-tuple-element.7), channel_id=1, source_target_pairs={{0,7},{1,0},{2,1},{3,2},{4,3},{5,4},{6,5},{7,6},{8,15},{9,8},{10,9... | collective-permute-start | bytes 393224 | tf_op jit(solution)/shard_map/ppermute | solution.py:364
  26.1 0.0 collective-permute-start.1
  26.1 2.5 %collective-permute-done = bf16[8,64,128]{2,1,0:T(8,128)(2,1)S(1)} collective-permute-done((bf16[8,64,128]{2,1,0:T(8,128)(2,1)S(1)}, bf16[8,64,128]{2,1,0:T(8,128)(2,1)S(1)}, u32[]{:S(2)}, u32[]{:S(2)}) %collective-permute-start) | collective-permute-done | bytes 131104 | tf_op jit(solution)/shard_map/ppermute | solution.py:364
  28.6 3.1 %collective-permute-done.1 = bf16[8,64,128]{2,1,0:T(8,128)(2,1)S(1)} collective-permute-done((bf16[8,64,128]{2,1,0:T(8,128)(2,1)S(1)}, bf16[8,64,128]{2,1,0:T(8,128)(2,1)S(1)}, u32[]{:S(2)}, u32[]{:S(2)}) %collective-permute-start.1) | collective-permute-done | bytes 131104 | tf_op jit(solution)/shard_map/ppermute | solution.py:364
  31.7 0.1 add_convert_fusion
  31.7 3.1 %collective-permute-start.2 = (bf16[4,64,128]{2,1,0:T(8,128)(2,1)S(1)}, bf16[4,64,128]{2,1,0:T(8,128)(2,1)S(1)}, u32[]{:S(2)}, u32[]{:S(2)}) collective-permute-start(bf16[4,64,128]{2,1,0:T(8,128)(2,1)S(1)} %slice.9), channel_id=1, source_target_pairs={{0,24},{8,0},{16,8},{24,16},{1,25},{9,1},{17,9},{25,17},{2,26},{10... | collective-permute-start | bytes 196616 | tf_op jit(solution)/shard_map/ppermute | solution.py:364
  34.8 0.0 copy-done
  34.8 0.0 copy-done.2
  34.8 0.0 copy-done.3
  34.8 0.4 kernel_order.1
  35.2 1.5 %collective-permute-done.2 = bf16[4,64,128]{2,1,0:T(8,128)(2,1)S(1)} collective-permute-done((bf16[4,64,128]{2,1,0:T(8,128)(2,1)S(1)}, bf16[4,64,128]{2,1,0:T(8,128)(2,1)S(1)}, u32[]{:S(2)}, u32[]{:S(2)}) %collective-permute-start.2) | collective-permute-done | bytes 65568 | tf_op jit(solution)/shard_map/ppermute | solution.py:364
  36.8 2.8 %collective-permute-start.5 = (bf16[5,64,128]{2,1,0:T(8,128)(2,1)S(1)}, bf16[5,64,128]{2,1,0:T(8,128)(2,1)S(1)}, u32[]{:S(2)}, u32[]{:S(2)}) collective-permute-start(bf16[5,64,128]{2,1,0:T(8,128)(2,1)S(1)} %pad_maximum_fusion.1.refs_0_), channel_id=1, source_target_pairs={{0,96},{32,0},{64,32},{96,64},{1,97},{33,1},{65,33},{97,65},{2,98}... | collective-permute-start | bytes 245768 | tf_op jit(solution)/shard_map/ppermute | solution.py:364
  39.6 0.8 %collective-permute-start.4 = (bf16[5,64,128]{2,1,0:T(8,128)(2,1)S(1)}, bf16[5,64,128]{2,1,0:T(8,128)(2,1)S(1)}, u32[]{:S(2)}, u32[]{:S(2)}) collective-permute-start(bf16[5,64,128]{2,1,0:T(8,128)(2,1)S(1)} %pad_maximum_fusion.1.refs_0_), channel_id=1, source_target_pairs={{0,64},{32,96},{64,0},{96,32},{1,65},{33,97},{65,1},{97,33},{2,66}... | collective-permute-start | bytes 245768 | tf_op jit(solution)/shard_map/ppermute | solution.py:364
  40.4 0.9 %collective-permute-start.3 = (bf16[5,64,128]{2,1,0:T(8,128)(2,1)S(1)}, bf16[5,64,128]{2,1,0:T(8,128)(2,1)S(1)}, u32[]{:S(2)}, u32[]{:S(2)}) collective-permute-start(bf16[5,64,128]{2,1,0:T(8,128)(2,1)S(1)} %pad_maximum_fusion.1.refs_0_), channel_id=1, source_target_pairs={{0,32},{32,64},{64,96},{96,0},{1,33},{33,65},{65,97},{97,1},{2,34}... | collective-permute-start | bytes 245768 | tf_op jit(solution)/shard_map/ppermute | solution.py:364
  41.3 0.4 collective-permute-done.5.refs_3_
  41.7 3.9 %collective-permute-done.4.refs_2_ = bf16[5,64,128]{2,1,0:T(8,128)(2,1)S(1)} collective-permute-done((bf16[5,64,128]{2,1,0:T(8,128)(2,1)S(1)}, bf16[5,64,128]{2,1,0:T(8,128)(2,1)S(1)}, u32[]{:S(2)}, u32[]{:S(2)}) %collective-permute-start.4) | collective-permute-done | bytes 81952 | tf_op jit(solution)/shard_map/ppermute | solution.py:364
  45.6 0.8 %collective-permute-done.3.refs_1_ = bf16[5,64,128]{2,1,0:T(8,128)(2,1)S(1)} collective-permute-done((bf16[5,64,128]{2,1,0:T(8,128)(2,1)S(1)}, bf16[5,64,128]{2,1,0:T(8,128)(2,1)S(1)}, u32[]{:S(2)}, u32[]{:S(2)}) %collective-permute-start.3) | collective-permute-done | bytes 81952 | tf_op jit(solution)/shard_map/ppermute | solution.py:364
  46.5 1.0 %collective-permute-start.6 = (bf16[4,64,128]{2,1,0:T(8,128)(2,1)S(1)}, bf16[4,64,128]{2,1,0:T(8,128)(2,1)S(1)}, u32[]{:S(2)}, u32[]{:S(2)}) collective-permute-start(bf16[4,64,128]{2,1,0:T(8,128)(2,1)S(1)} %potential.1.pot), channel_id=1, source_target_pairs={{0,8},{8,16},{16,24},{24,0},{1,9},{9,17},{17,25},{25,1},{2,10},{10... | collective-permute-start | bytes 196616 | tf_op jit(solution)/shard_map/ppermute | solution.py:364
  47.5 4.9 %collective-permute-done.6 = bf16[4,64,128]{2,1,0:T(8,128)(2,1)S(1)} collective-permute-done((bf16[4,64,128]{2,1,0:T(8,128)(2,1)S(1)}, bf16[4,64,128]{2,1,0:T(8,128)(2,1)S(1)}, u32[]{:S(2)}, u32[]{:S(2)}) %collective-permute-start.6) | collective-permute-done | bytes 65568 | tf_op jit(solution)/shard_map/ppermute | solution.py:364
  52.4 0.0 collective-permute-start.8
  52.4 0.5 collective-permute-start.7
  52.9 0.3 natural_order.1
  53.3 0.7 copy.17
  53.9 1.0 %collective-permute-done.8.pot2 = bf16[8,64,128]{2,1,0:T(8,128)(2,1)S(1)} collective-permute-done((bf16[8,64,128]{2,1,0:T(8,128)(2,1)S(1)}, bf16[8,64,128]{2,1,0:T(8,128)(2,1)S(1)}, u32[]{:S(2)}, u32[]{:S(2)}) %collective-permute-start.8) | collective-permute-done | bytes 131104 | tf_op jit(solution)/shard_map/ppermute | solution.py:364
  54.9 3.1 %collective-permute-done.7.pot0 = bf16[8,64,128]{2,1,0:T(8,128)(2,1)S(1)} collective-permute-done((bf16[8,64,128]{2,1,0:T(8,128)(2,1)S(1)}, bf16[8,64,128]{2,1,0:T(8,128)(2,1)S(1)}, u32[]{:S(2)}, u32[]{:S(2)}) %collective-permute-start.7) | collective-permute-done | bytes 131104 | tf_op jit(solution)/shard_map/ppermute | solution.py:364
  58.0 0.0 copy-done.1
  58.0 0.0 copy-done.4
  58.0 11.8 %box_apply.1 = bf16[80,256,128]{2,1,0:T(8,128)(2,1)} custom-call(s32[1]{0:T(128)} %bitcast.at_y, s32[1]{0:T(128)} %bitcast.1.at_z, s32[80]{0:T(128)} %bitcast.36, bf16[8,64,128]{2,1,0:T(8,128)(2,1)S(1)} %collective-permute-done.7.pot0, bf16[8,64,128]{2,1,0:T(8,128)(2,1)S(1)} %pad_maximum_fusion.pot1, bf16[8,64,128]{2,1,0:T(8,128)(2,1)S(1)} %collective-permute-done.8.pot2, ...), custom_call_target="tpu_custom_call" | custom-call | flops 1000000000 | bytes 27000000 | tf_op jit(solution)/shard_map/box_apply/pallas_call | solution.py:296
  (5 shorter events, 0.1 us)
Async XLA Ops:
  0.6 34.2 %copy-start = (f32[128,128]{1,0:T(8,128)S(1)}, f32[128,128]{1,0:T(8,128)}, u32[]{:S(2)}) copy-start(f32[128,128]{1,0:T(8,128)} %constant.30.clone.cols) | copy-start | bytes 196612
  0.6 34.2 %copy-start.2 = (f32[64,64]{1,0:T(8,128)S(1)}, f32[64,64]{1,0:T(8,128)}, u32[]{:S(2)}) copy-start(f32[64,64]{1,0:T(8,128)} %constant.29.clone.rows) | copy-start | bytes 49156
  0.7 34.2 %copy-start.3 = (f32[1,8192]{1,0:T(1,128)S(1)}, f32[1,8192]{1,0:T(1,128)}, u32[]{:S(2)}) copy-start(f32[1,8192]{1,0:T(1,128)} %param.18) | copy-start | bytes 98308
  0.7 57.4 %copy-start.1 = (bf16[256,256]{1,0:T(8,128)(2,1)S(1)}, bf16[256,256]{1,0:T(8,128)(2,1)}, u32[]{:S(2)}) copy-start(bf16[256,256]{1,0:T(8,128)(2,1)} %constant.32.clone.wide_t) | copy-start | bytes 393220
  0.7 57.3 %copy-start.4 = (bf16[64,64]{1,0:T(8,128)(2,1)S(1)}, bf16[64,64]{1,0:T(8,128)(2,1)}, u32[]{:S(2)}) copy-start(bf16[64,64]{1,0:T(8,128)(2,1)} %constant.31.clone.odd_xt) | copy-start | bytes 24580
  22.5 6.1 %collective-permute-start = (bf16[8,64,128]{2,1,0:T(8,128)(2,1)S(1)}, bf16[8,64,128]{2,1,0:T(8,128)(2,1)S(1)}, u32[]{:S(2)}, u32[]{:S(2)}) collective-permute-start(bf16[8,64,128]{2,1,0:T(8,128)(2,1)S(1)} %get-tuple-element.7), channel_id=1, source_target_pairs={{0,7},{1,0},{2,1},{3,2},{4,3},{5,4},{6,5},{7,6},{8,15},{9,8},{10,9... | collective-permute-start | bytes 393224 | tf_op jit(solution)/shard_map/ppermute | solution.py:364
  26.1 5.6 %collective-permute-start.1 = (bf16[8,64,128]{2,1,0:T(8,128)(2,1)S(1)}, bf16[8,64,128]{2,1,0:T(8,128)(2,1)S(1)}, u32[]{:S(2)}, u32[]{:S(2)}) collective-permute-start(bf16[8,64,128]{2,1,0:T(8,128)(2,1)S(1)} %get-tuple-element.8), channel_id=1, source_target_pairs={{0,1},{1,2},{2,3},{3,4},{4,5},{5,6},{6,7},{7,0},{8,9},{9,10},{10,1... | collective-permute-start | bytes 393224 | tf_op jit(solution)/shard_map/ppermute | solution.py:364
  31.7 5.0 %collective-permute-start.2 = (bf16[4,64,128]{2,1,0:T(8,128)(2,1)S(1)}, bf16[4,64,128]{2,1,0:T(8,128)(2,1)S(1)}, u32[]{:S(2)}, u32[]{:S(2)}) collective-permute-start(bf16[4,64,128]{2,1,0:T(8,128)(2,1)S(1)} %slice.9), channel_id=1, source_target_pairs={{0,24},{8,0},{16,8},{24,16},{1,25},{9,1},{17,9},{25,17},{2,26},{10... | collective-permute-start | bytes 196616 | tf_op jit(solution)/shard_map/ppermute | solution.py:364
  36.8 4.9 %collective-permute-start.5 = (bf16[5,64,128]{2,1,0:T(8,128)(2,1)S(1)}, bf16[5,64,128]{2,1,0:T(8,128)(2,1)S(1)}, u32[]{:S(2)}, u32[]{:S(2)}) collective-permute-start(bf16[5,64,128]{2,1,0:T(8,128)(2,1)S(1)} %pad_maximum_fusion.1.refs_0_), channel_id=1, source_target_pairs={{0,96},{32,0},{64,32},{96,64},{1,97},{33,1},{65,33},{97,65},{2,98}... | collective-permute-start | bytes 245768 | tf_op jit(solution)/shard_map/ppermute | solution.py:364
  39.6 6.0 %collective-permute-start.4 = (bf16[5,64,128]{2,1,0:T(8,128)(2,1)S(1)}, bf16[5,64,128]{2,1,0:T(8,128)(2,1)S(1)}, u32[]{:S(2)}, u32[]{:S(2)}) collective-permute-start(bf16[5,64,128]{2,1,0:T(8,128)(2,1)S(1)} %pad_maximum_fusion.1.refs_0_), channel_id=1, source_target_pairs={{0,64},{32,96},{64,0},{96,32},{1,65},{33,97},{65,1},{97,33},{2,66}... | collective-permute-start | bytes 245768 | tf_op jit(solution)/shard_map/ppermute | solution.py:364
  40.4 6.0 %collective-permute-start.3 = (bf16[5,64,128]{2,1,0:T(8,128)(2,1)S(1)}, bf16[5,64,128]{2,1,0:T(8,128)(2,1)S(1)}, u32[]{:S(2)}, u32[]{:S(2)}) collective-permute-start(bf16[5,64,128]{2,1,0:T(8,128)(2,1)S(1)} %pad_maximum_fusion.1.refs_0_), channel_id=1, source_target_pairs={{0,32},{32,64},{64,96},{96,0},{1,33},{33,65},{65,97},{97,1},{2,34}... | collective-permute-start | bytes 245768 | tf_op jit(solution)/shard_map/ppermute | solution.py:364
  46.5 5.9 %collective-permute-start.6 = (bf16[4,64,128]{2,1,0:T(8,128)(2,1)S(1)}, bf16[4,64,128]{2,1,0:T(8,128)(2,1)S(1)}, u32[]{:S(2)}, u32[]{:S(2)}) collective-permute-start(bf16[4,64,128]{2,1,0:T(8,128)(2,1)S(1)} %potential.1.pot), channel_id=1, source_target_pairs={{0,8},{8,16},{16,24},{24,0},{1,9},{9,17},{17,25},{25,1},{2,10},{10... | collective-permute-start | bytes 196616 | tf_op jit(solution)/shard_map/ppermute | solution.py:364
  52.4 2.5 %collective-permute-start.8 = (bf16[8,64,128]{2,1,0:T(8,128)(2,1)S(1)}, bf16[8,64,128]{2,1,0:T(8,128)(2,1)S(1)}, u32[]{:S(2)}, u32[]{:S(2)}) collective-permute-start(bf16[8,64,128]{2,1,0:T(8,128)(2,1)S(1)} %pad_maximum_fusion.pot1), channel_id=1, source_target_pairs={{0,7},{1,0},{2,1},{3,2},{4,3},{5,4},{6,5},{7,6},{8,15},{9,8},{10,9... | collective-permute-start | bytes 393224 | tf_op jit(solution)/shard_map/ppermute | solution.py:364
  52.4 5.6 %collective-permute-start.7 = (bf16[8,64,128]{2,1,0:T(8,128)(2,1)S(1)}, bf16[8,64,128]{2,1,0:T(8,128)(2,1)S(1)}, u32[]{:S(2)}, u32[]{:S(2)}) collective-permute-start(bf16[8,64,128]{2,1,0:T(8,128)(2,1)S(1)} %pad_maximum_fusion.pot1), channel_id=1, source_target_pairs={{0,1},{1,2},{2,3},{3,4},{4,5},{5,6},{6,7},{7,0},{8,9},{9,10},{10,1... | collective-permute-start | bytes 393224 | tf_op jit(solution)/shard_map/ppermute | solution.py:364

commit v4 on v3

--- a/solution.py
+++ b/solution.py
@@ -8,8 +8,9 @@
 from jax.sharding import PartitionSpec as P
 
 AXES = ("gx", "gy", "gz")
-GROUP = 16
-HELD = 8
+GROUP = 20
+HELD = 10
+SENT = 4
 SLOTS = 4
 BF16 = jnp.bfloat16
 F32 = jnp.float32
@@ -62,8 +63,20 @@
                 stage(t - lag * i)
 
 
-def density_kernel(at_y, at_z, domains, func, resp, pidx, pw, spread, odd_x, wide, part0, part1, part2, fine, acc, stage, mixer, rs):
+def density_kernel(at_y, at_z, domains, func, resp, pidx, pw, spread, odd_x, wide, part0, part1, part2, fine, acc, stage, mixer, rs, held, sems):
     step = pl.program_id(0)
+    parity = lax.rem(step, 2)
+
+    def send(i, b):
+        slot = lax.rem(i, 2)
+        there = fine.at[pl.ds(i * GROUP + b, SENT)]
+        return pltpu.make_async_copy(held.at[slot, pl.ds(b, SENT)], there, sems.at[slot, b // SENT])
+
+    @pl.when(step >= 2)
+    def _():
+        for b in range(0, GROUP, SENT):
+            send(step - 2, b).wait()
+
     rows8 = 8 * GROUP
 
     @pl.when(step == 0)
@@ -98,7 +111,7 @@
     )
 
     def place(which, b):
-        return fine.at[b, 0] if which == 0 else rs.at[b]
+        return held.at[parity, b, 0] if which == 0 else rs.at[b]
 
     def mix(b):
         pairs = mixer[pl.ds(pl.multiple_of((step * GROUP + b) * 8, 8), 8), :]
@@ -131,11 +144,13 @@
                 to[128 * i + 64 : 128 * i + 128, :] = odd.astype(BF16)
 
     def along_y(b):
-        tall_f = fine[b, 0]
+        tall_f = held[parity, b, 0]
         tall_r = rs[b]
         shift_f = jnp.dot(tall_f, wide[...], preferred_element_type=F32).astype(BF16)
         shift_r = jnp.dot(tall_r, wide[...], preferred_element_type=F32).astype(BF16)
-        fine[b, 1] = shift_f
+        held[parity, b, 1] = shift_f
+        if b % SENT == SENT - 1:
+            send(step, b + 1 - SENT).start()
         s0, s1 = slots_of((at_y[0], at_z[0]), domains[step * GROUP + b])
         for par, den in ((0, tall_f * tall_r), (1, shift_f * shift_r)):
             den = den[:128] + den[128:]
@@ -157,6 +172,9 @@
 
         for d in range(24):
             fold(d, 0)
+        for i in (step - 1, step):
+            for b in range(0, GROUP, SENT):
+                send(i, b).wait()
 
 
 def as_tiles(array):
@@ -194,13 +212,15 @@
             ],
             out_specs=[
                 *[pl.BlockSpec((8, 64, 128), lambda i, *_: (0, 0, 0))] * 3,
-                pl.BlockSpec((GROUP, 2, 256, 256), lambda i, *_: (i, 0, 0, 0)),
+                pl.BlockSpec(memory_space=pl.ANY),
             ],
             scratch_shapes=[
                 pltpu.VMEM((24, 2, 64, 128), F32),
                 pltpu.VMEM((2, GROUP, 256, 128), F32),
                 pltpu.VMEM((8 * boxes, 128), F32),
                 pltpu.VMEM((GROUP, 256, 256), BF16),
+                pltpu.VMEM((2, GROUP, 2, 256, 256), BF16),
+                pltpu.SemaphoreType.DMA((2, GROUP // SENT)),
             ],
         ),
         out_shape=[

time: 70.1 us -> 67.9 us (0.969)
  Pallas kernels: 34.4 us -> 32.3 us
    pallas_call x1, Pallas kernels: 21.8 us -> 20.1 us  [box_density(): pl.pallas_call(density_kernel, grid_spec=pltpu.PrefetchScalarGridSpec(num...]
where the time goes in v4:
time: 67.9 us; the launch traced here: 67.8 us
  Pallas kernels  32.3 us (48%)
  waiting for transfers between devices  21.2 us (31%)
  starting transfers between devices  12.7 us (19%)
  between operations  0.74 us (1%)
  local copies, waits for them, and re-layouts  0.69 us (1%)
    ppermute x9, waiting for transfers between devices, shifted(): lax.ppermute(array, axis, [(i, (i + by) % size) for i in range(size)])  21.2 us
    pallas_call x1, Pallas kernels, box_density(): pl.pallas_call(density_kernel, grid_spec=pltpu.PrefetchScalarGridSpec(num...  20.1 us
    ppermute x9, starting transfers between devices, shifted(): lax.ppermute(array, axis, [(i, (i + by) % size) for i in range(size)])  12.7 us
    pallas_call x1, Pallas kernels, box_apply(): pl.pallas_call(apply_kernel, grid_spec=pltpu.PrefetchScalarGridSpec(num_s...  11.5 us
  transfers between devices with their start and end apart: 9, of which 9 were waited for; matrix products, arithmetic and copies ran while one was open for 1% of the time, Pallas kernels for 1%

profile of v4, /device:TPU:0, one launch (start us, length us, event | category | flops | bytes accessed | tf_op | source)
XLA Modules:
  0.0 67.8 jit_solution(16120056422300916765)
XLA Ops:
  0.6 0.0 copy-start
  0.6 0.0 copy-start.2
  0.7 0.0 copy-start.3
  0.7 0.0 copy-start.1
  0.7 0.0 copy-start.4
  0.7 20.1 %box_density.1 = (bf16[8,64,128]{2,1,0:T(8,128)(2,1)S(1)}, bf16[8,64,128]{2,1,0:T(8,128)(2,1)S(1)}, bf16[8,64,128]{2,1,0:T(8,128)(2,1)S(1)}, bf16[80,2,256,256]{3,2,1,0:T(8,128)(2,1)}) custom-call(s32[1]{0:T(128)} %bitcast.at_y, s32[1]{0:T(128)} %bitcast.1.at_z, s32[80]{0:T(128)} %bitcast.35, bf16[80,256,128]{2,1,0:T(8,128)(2,1)} %bitcast.29, ...), custom_call_target="tpu_custom_call" | custom-call | flops 2000000000 | bytes 32000000 | tf_op jit(solution)/shard_map/box_density/pallas_call | solution.py:199
  20.8 3.6 %collective-permute-start = (bf16[8,64,128]{2,1,0:T(8,128)(2,1)S(1)}, bf16[8,64,128]{2,1,0:T(8,128)(2,1)S(1)}, u32[]{:S(2)}, u32[]{:S(2)}) collective-permute-start(bf16[8,64,128]{2,1,0:T(8,128)(2,1)S(1)} %get-tuple-element.7), channel_id=1, source_target_pairs={{0,7},{1,0},{2,1},{3,2},{4,3},{5,4},{6,5},{7,6},{8,15},{9,8},{10,9... | collective-permute-start | bytes 393224 | tf_op jit(solution)/shard_map/ppermute | solution.py:384
  24.3 0.0 collective-permute-start.1
  24.3 2.5 %collective-permute-done = bf16[8,64,128]{2,1,0:T(8,128)(2,1)S(1)} collective-permute-done((bf16[8,64,128]{2,1,0:T(8,128)(2,1)S(1)}, bf16[8,64,128]{2,1,0:T(8,128)(2,1)S(1)}, u32[]{:S(2)}, u32[]{:S(2)}) %collective-permute-start) | collective-permute-done | bytes 131104 | tf_op jit(solution)/shard_map/ppermute | solution.py:384
  26.9 3.1 %collective-permute-done.1 = bf16[8,64,128]{2,1,0:T(8,128)(2,1)S(1)} collective-permute-done((bf16[8,64,128]{2,1,0:T(8,128)(2,1)S(1)}, bf16[8,64,128]{2,1,0:T(8,128)(2,1)S(1)}, u32[]{:S(2)}, u32[]{:S(2)}) %collective-permute-start.1) | collective-permute-done | bytes 131104 | tf_op jit(solution)/shard_map/ppermute | solution.py:384
  29.9 0.1 add_convert_fusion
  30.0 3.1 %collective-permute-start.2 = (bf16[4,64,128]{2,1,0:T(8,128)(2,1)S(1)}, bf16[4,64,128]{2,1,0:T(8,128)(2,1)S(1)}, u32[]{:S(2)}, u32[]{:S(2)}) collective-permute-start(bf16[4,64,128]{2,1,0:T(8,128)(2,1)S(1)} %slice.9), channel_id=1, source_target_pairs={{0,24},{8,0},{16,8},{24,16},{1,25},{9,1},{17,9},{25,17},{2,26},{10... | collective-permute-start | bytes 196616 | tf_op jit(solution)/shard_map/ppermute | solution.py:384
  33.1 0.0 copy-done
  33.1 0.0 copy-done.2
  33.1 0.0 copy-done.3
  33.1 0.4 kernel_order.1
  33.5 1.5 %collective-permute-done.2 = bf16[4,64,128]{2,1,0:T(8,128)(2,1)S(1)} collective-permute-done((bf16[4,64,128]{2,1,0:T(8,128)(2,1)S(1)}, bf16[4,64,128]{2,1,0:T(8,128)(2,1)S(1)}, u32[]{:S(2)}, u32[]{:S(2)}) %collective-permute-start.2) | collective-permute-done | bytes 65568 | tf_op jit(solution)/shard_map/ppermute | solution.py:384
  35.1 2.8 %collective-permute-start.5 = (bf16[5,64,128]{2,1,0:T(8,128)(2,1)S(1)}, bf16[5,64,128]{2,1,0:T(8,128)(2,1)S(1)}, u32[]{:S(2)}, u32[]{:S(2)}) collective-permute-start(bf16[5,64,128]{2,1,0:T(8,128)(2,1)S(1)} %pad_maximum_fusion.1.refs_0_), channel_id=1, source_target_pairs={{0,96},{32,0},{64,32},{96,64},{1,97},{33,1},{65,33},{97,65},{2,98}... | collective-permute-start | bytes 245768 | tf_op jit(solution)/shard_map/ppermute | solution.py:384
  37.9 0.8 %collective-permute-start.4 = (bf16[5,64,128]{2,1,0:T(8,128)(2,1)S(1)}, bf16[5,64,128]{2,1,0:T(8,128)(2,1)S(1)}, u32[]{:S(2)}, u32[]{:S(2)}) collective-permute-start(bf16[5,64,128]{2,1,0:T(8,128)(2,1)S(1)} %pad_maximum_fusion.1.refs_0_), channel_id=1, source_target_pairs={{0,64},{32,96},{64,0},{96,32},{1,65},{33,97},{65,1},{97,33},{2,66}... | collective-permute-start | bytes 245768 | tf_op jit(solution)/shard_map/ppermute | solution.py:384
  38.7 0.9 %collective-permute-start.3 = (bf16[5,64,128]{2,1,0:T(8,128)(2,1)S(1)}, bf16[5,64,128]{2,1,0:T(8,128)(2,1)S(1)}, u32[]{:S(2)}, u32[]{:S(2)}) collective-permute-start(bf16[5,64,128]{2,1,0:T(8,128)(2,1)S(1)} %pad_maximum_fusion.1.refs_0_), channel_id=1, source_target_pairs={{0,32},{32,64},{64,96},{96,0},{1,33},{33,65},{65,97},{97,1},{2,34}... | collective-permute-start | bytes 245768 | tf_op jit(solution)/shard_map/ppermute | solution.py:384
  39.6 0.4 collective-permute-done.5.refs_3_
  39.9 3.9 %collective-permute-done.4.refs_2_ = bf16[5,64,128]{2,1,0:T(8,128)(2,1)S(1)} collective-permute-done((bf16[5,64,128]{2,1,0:T(8,128)(2,1)S(1)}, bf16[5,64,128]{2,1,0:T(8,128)(2,1)S(1)}, u32[]{:S(2)}, u32[]{:S(2)}) %collective-permute-start.4) | collective-permute-done | bytes 81952 | tf_op jit(solution)/shard_map/ppermute | solution.py:384
  43.9 0.8 %collective-permute-done.3.refs_1_ = bf16[5,64,128]{2,1,0:T(8,128)(2,1)S(1)} collective-permute-done((bf16[5,64,128]{2,1,0:T(8,128)(2,1)S(1)}, bf16[5,64,128]{2,1,0:T(8,128)(2,1)S(1)}, u32[]{:S(2)}, u32[]{:S(2)}) %collective-permute-start.3) | collective-permute-done | bytes 81952 | tf_op jit(solution)/shard_map/ppermute | solution.py:384
  44.8 1.0 %collective-permute-start.6 = (bf16[4,64,128]{2,1,0:T(8,128)(2,1)S(1)}, bf16[4,64,128]{2,1,0:T(8,128)(2,1)S(1)}, u32[]{:S(2)}, u32[]{:S(2)}) collective-permute-start(bf16[4,64,128]{2,1,0:T(8,128)(2,1)S(1)} %potential.1.pot), channel_id=1, source_target_pairs={{0,8},{8,16},{16,24},{24,0},{1,9},{9,17},{17,25},{25,1},{2,10},{10... | collective-permute-start | bytes 196616 | tf_op jit(solution)/shard_map/ppermute | solution.py:384
  45.7 4.9 %collective-permute-done.6 = bf16[4,64,128]{2,1,0:T(8,128)(2,1)S(1)} collective-permute-done((bf16[4,64,128]{2,1,0:T(8,128)(2,1)S(1)}, bf16[4,64,128]{2,1,0:T(8,128)(2,1)S(1)}, u32[]{:S(2)}, u32[]{:S(2)}) %collective-permute-start.6) | collective-permute-done | bytes 65568 | tf_op jit(solution)/shard_map/ppermute | solution.py:384
  50.7 0.0 collective-permute-start.8
  50.7 0.5 collective-permute-start.7
  51.2 0.3 natural_order.1
  51.5 0.7 copy.17
  52.2 1.0 %collective-permute-done.8.pot2 = bf16[8,64,128]{2,1,0:T(8,128)(2,1)S(1)} collective-permute-done((bf16[8,64,128]{2,1,0:T(8,128)(2,1)S(1)}, bf16[8,64,128]{2,1,0:T(8,128)(2,1)S(1)}, u32[]{:S(2)}, u32[]{:S(2)}) %collective-permute-start.8) | collective-permute-done | bytes 131104 | tf_op jit(solution)/shard_map/ppermute | solution.py:384
  53.2 3.1 %collective-permute-done.7.pot0 = bf16[8,64,128]{2,1,0:T(8,128)(2,1)S(1)} collective-permute-done((bf16[8,64,128]{2,1,0:T(8,128)(2,1)S(1)}, bf16[8,64,128]{2,1,0:T(8,128)(2,1)S(1)}, u32[]{:S(2)}, u32[]{:S(2)}) %collective-permute-start.7) | collective-permute-done | bytes 131104 | tf_op jit(solution)/shard_map/ppermute | solution.py:384
  56.3 0.0 copy-done.1
  56.3 0.0 copy-done.4
  56.3 11.5 %box_apply.1 = bf16[80,256,128]{2,1,0:T(8,128)(2,1)} custom-call(s32[1]{0:T(128)} %bitcast.at_y, s32[1]{0:T(128)} %bitcast.1.at_z, s32[80]{0:T(128)} %bitcast.36, bf16[8,64,128]{2,1,0:T(8,128)(2,1)S(1)} %collective-permute-done.7.pot0, bf16[8,64,128]{2,1,0:T(8,128)(2,1)S(1)} %pad_maximum_fusion.pot1, bf16[8,64,128]{2,1,0:T(8,128)(2,1)S(1)} %collective-permute-done.8.pot2, ...), custom_call_target="tpu_custom_call" | custom-call | flops 1000000000 | bytes 27000000 | tf_op jit(solution)/shard_map/box_apply/pallas_call | solution.py:316
  (5 shorter events, 0.1 us)
Async XLA Ops:
  0.6 32.5 %copy-start = (f32[128,128]{1,0:T(8,128)S(1)}, f32[128,128]{1,0:T(8,128)}, u32[]{:S(2)}) copy-start(f32[128,128]{1,0:T(8,128)} %constant.30.clone.cols) | copy-start | bytes 196612
  0.6 32.5 %copy-start.2 = (f32[64,64]{1,0:T(8,128)S(1)}, f32[64,64]{1,0:T(8,128)}, u32[]{:S(2)}) copy-start(f32[64,64]{1,0:T(8,128)} %constant.29.clone.rows) | copy-start | bytes 49156
  0.7 32.5 %copy-start.3 = (f32[1,8192]{1,0:T(1,128)S(1)}, f32[1,8192]{1,0:T(1,128)}, u32[]{:S(2)}) copy-start(f32[1,8192]{1,0:T(1,128)} %param.18) | copy-start | bytes 98308
  0.7 55.6 %copy-start.1 = (bf16[256,256]{1,0:T(8,128)(2,1)S(1)}, bf16[256,256]{1,0:T(8,128)(2,1)}, u32[]{:S(2)}) copy-start(bf16[256,256]{1,0:T(8,128)(2,1)} %constant.32.clone.wide_t) | copy-start | bytes 393220
  0.7 55.6 %copy-start.4 = (bf16[64,64]{1,0:T(8,128)(2,1)S(1)}, bf16[64,64]{1,0:T(8,128)(2,1)}, u32[]{:S(2)}) copy-start(bf16[64,64]{1,0:T(8,128)(2,1)} %constant.31.clone.odd_xt) | copy-start | bytes 24580
  20.8 6.1 %collective-permute-start = (bf16[8,64,128]{2,1,0:T(8,128)(2,1)S(1)}, bf16[8,64,128]{2,1,0:T(8,128)(2,1)S(1)}, u32[]{:S(2)}, u32[]{:S(2)}) collective-permute-start(bf16[8,64,128]{2,1,0:T(8,128)(2,1)S(1)} %get-tuple-element.7), channel_id=1, source_target_pairs={{0,7},{1,0},{2,1},{3,2},{4,3},{5,4},{6,5},{7,6},{8,15},{9,8},{10,9... | collective-permute-start | bytes 393224 | tf_op jit(solution)/shard_map/ppermute | solution.py:384
  24.3 5.6 %collective-permute-start.1 = (bf16[8,64,128]{2,1,0:T(8,128)(2,1)S(1)}, bf16[8,64,128]{2,1,0:T(8,128)(2,1)S(1)}, u32[]{:S(2)}, u32[]{:S(2)}) collective-permute-start(bf16[8,64,128]{2,1,0:T(8,128)(2,1)S(1)} %get-tuple-element.8), channel_id=1, source_target_pairs={{0,1},{1,2},{2,3},{3,4},{4,5},{5,6},{6,7},{7,0},{8,9},{9,10},{10,1... | collective-permute-start | bytes 393224 | tf_op jit(solution)/shard_map/ppermute | solution.py:384
  30.0 5.0 %collective-permute-start.2 = (bf16[4,64,128]{2,1,0:T(8,128)(2,1)S(1)}, bf16[4,64,128]{2,1,0:T(8,128)(2,1)S(1)}, u32[]{:S(2)}, u32[]{:S(2)}) collective-permute-start(bf16[4,64,128]{2,1,0:T(8,128)(2,1)S(1)} %slice.9), channel_id=1, source_target_pairs={{0,24},{8,0},{16,8},{24,16},{1,25},{9,1},{17,9},{25,17},{2,26},{10... | collective-permute-start | bytes 196616 | tf_op jit(solution)/shard_map/ppermute | solution.py:384
  35.1 4.9 %collective-permute-start.5 = (bf16[5,64,128]{2,1,0:T(8,128)(2,1)S(1)}, bf16[5,64,128]{2,1,0:T(8,128)(2,1)S(1)}, u32[]{:S(2)}, u32[]{:S(2)}) collective-permute-start(bf16[5,64,128]{2,1,0:T(8,128)(2,1)S(1)} %pad_maximum_fusion.1.refs_0_), channel_id=1, source_target_pairs={{0,96},{32,0},{64,32},{96,64},{1,97},{33,1},{65,33},{97,65},{2,98}... | collective-permute-start | bytes 245768 | tf_op jit(solution)/shard_map/ppermute | solution.py:384
  37.9 6.0 %collective-permute-start.4 = (bf16[5,64,128]{2,1,0:T(8,128)(2,1)S(1)}, bf16[5,64,128]{2,1,0:T(8,128)(2,1)S(1)}, u32[]{:S(2)}, u32[]{:S(2)}) collective-permute-start(bf16[5,64,128]{2,1,0:T(8,128)(2,1)S(1)} %pad_maximum_fusion.1.refs_0_), channel_id=1, source_target_pairs={{0,64},{32,96},{64,0},{96,32},{1,65},{33,97},{65,1},{97,33},{2,66}... | collective-permute-start | bytes 245768 | tf_op jit(solution)/shard_map/ppermute | solution.py:384
  38.7 6.0 %collective-permute-start.3 = (bf16[5,64,128]{2,1,0:T(8,128)(2,1)S(1)}, bf16[5,64,128]{2,1,0:T(8,128)(2,1)S(1)}, u32[]{:S(2)}, u32[]{:S(2)}) collective-permute-start(bf16[5,64,128]{2,1,0:T(8,128)(2,1)S(1)} %pad_maximum_fusion.1.refs_0_), channel_id=1, source_target_pairs={{0,32},{32,64},{64,96},{96,0},{1,33},{33,65},{65,97},{97,1},{2,34}... | collective-permute-start | bytes 245768 | tf_op jit(solution)/shard_map/ppermute | solution.py:384
  44.8 5.9 %collective-permute-start.6 = (bf16[4,64,128]{2,1,0:T(8,128)(2,1)S(1)}, bf16[4,64,128]{2,1,0:T(8,128)(2,1)S(1)}, u32[]{:S(2)}, u32[]{:S(2)}) collective-permute-start(bf16[4,64,128]{2,1,0:T(8,128)(2,1)S(1)} %potential.1.pot), channel_id=1, source_target_pairs={{0,8},{8,16},{16,24},{24,0},{1,9},{9,17},{17,25},{25,1},{2,10},{10... | collective-permute-start | bytes 196616 | tf_op jit(solution)/shard_map/ppermute | solution.py:384
  50.7 2.5 %collective-permute-start.8 = (bf16[8,64,128]{2,1,0:T(8,128)(2,1)S(1)}, bf16[8,64,128]{2,1,0:T(8,128)(2,1)S(1)}, u32[]{:S(2)}, u32[]{:S(2)}) collective-permute-start(bf16[8,64,128]{2,1,0:T(8,128)(2,1)S(1)} %pad_maximum_fusion.pot1), channel_id=1, source_target_pairs={{0,7},{1,0},{2,1},{3,2},{4,3},{5,4},{6,5},{7,6},{8,15},{9,8},{10,9... | collective-permute-start | bytes 393224 | tf_op jit(solution)/shard_map/ppermute | solution.py:384
  50.7 5.6 %collective-permute-start.7 = (bf16[8,64,128]{2,1,0:T(8,128)(2,1)S(1)}, bf16[8,64,128]{2,1,0:T(8,128)(2,1)S(1)}, u32[]{:S(2)}, u32[]{:S(2)}) collective-permute-start(bf16[8,64,128]{2,1,0:T(8,128)(2,1)S(1)} %pad_maximum_fusion.pot1), channel_id=1, source_target_pairs={{0,1},{1,2},{2,3},{3,4},{4,5},{5,6},{6,7},{7,0},{8,9},{9,10},{10,1... | collective-permute-start | bytes 393224 | tf_op jit(solution)/shard_map/ppermute | solution.py:384

commit v5 on v4

--- a/solution.py
+++ b/solution.py
@@ -83,11 +83,11 @@
     def _():
         acc[...] = jnp.zeros_like(acc)
 
-        def widen(a, precision=None):
-            return jnp.dot(a, spread[...], precision=precision, preferred_element_type=F32)
+        def widen(a):
+            return jnp.dot(a.astype(BF16), spread[...], preferred_element_type=F32)
 
         level = (lax.broadcasted_iota(jnp.int32, (24, 640), 1) % 8).astype(F32)
-        weight = widen(pw[...], lax.Precision.HIGHEST)
+        weight = widen(pw[...])
         first = jnp.where(widen(pidx[0].astype(F32)) == level, weight, 0.0)
         second = jnp.where(widen(pidx[1].astype(F32)) == level, 1.0, 0.0)
         at_row = lax.broadcasted_iota(jnp.int32, (128, 128), 0)
@@ -96,10 +96,9 @@
         for i in range(5):
             cut = slice(128 * i, 128 * i + 128)
             cross = lax.dot_general(
-                first[:, cut],
-                second[:, cut],
+                first[:, cut].astype(BF16),
+                second[:, cut].astype(BF16),
                 (((0,), (0,)), ((), ())),
-                precision=lax.Precision.HIGHEST,
                 preferred_element_type=F32,
             )
             cross = jnp.where(at_row // 8 == at_col // 8, cross, 0.0).astype(BF16)
@@ -186,7 +185,7 @@
     boxes = functions.shape[0]
     odd_x, wide = tables()
     steps = boxes // GROUP
-    spread = np.repeat(np.eye(boxes, dtype=np.float32), 8, axis=1)
+    spread = np.repeat(np.eye(boxes), 8, axis=1).astype(ml_dtypes.bfloat16)
     arrays = (
         as_tiles(functions),
         as_tiles(responses),

time: 67.9 us -> 66.9 us (0.985)
  Pallas kernels: 32.3 us -> 31.4 us
    pallas_call x1, Pallas kernels: 20.1 us -> 19.1 us  [box_density(): pl.pallas_call(density_kernel, grid_spec=pltpu.PrefetchScalarGridSpec(num...]
where the time goes in v5:
time: 66.9 us; the launch traced here: 66.8 us
  Pallas kernels  31.4 us (47%)
  waiting for transfers between devices  21.2 us (32%)
  starting transfers between devices  12.7 us (19%)
  between operations  0.74 us (1%)
  local copies, waits for them, and re-layouts  0.69 us (1%)
    ppermute x9, waiting for transfers between devices, shifted(): lax.ppermute(array, axis, [(i, (i + by) % size) for i in range(size)])  21.2 us
    pallas_call x1, Pallas kernels, box_density(): pl.pallas_call(density_kernel, grid_spec=pltpu.PrefetchScalarGridSpec(num...  19.1 us
    ppermute x9, starting transfers between devices, shifted(): lax.ppermute(array, axis, [(i, (i + by) % size) for i in range(size)])  12.7 us
    pallas_call x1, Pallas kernels, box_apply(): pl.pallas_call(apply_kernel, grid_spec=pltpu.PrefetchScalarGridSpec(num_s...  11.5 us
  transfers between devices with their start and end apart: 9, of which 9 were waited for; matrix products, arithmetic and copies ran while one was open for 1% of the time, Pallas kernels for 1%

profile of v5, /device:TPU:0, one launch (start us, length us, event | category | flops | bytes accessed | tf_op | source)
XLA Modules:
  0.0 66.8 jit_solution(15428918800798725282)
XLA Ops:
  0.6 0.0 copy-start
  0.6 0.0 copy-start.2
  0.7 0.0 copy-start.3
  0.7 0.0 copy-start.1
  0.7 0.0 copy-start.4
  0.7 19.1 %box_density.1 = (bf16[8,64,128]{2,1,0:T(8,128)(2,1)S(1)}, bf16[8,64,128]{2,1,0:T(8,128)(2,1)S(1)}, bf16[8,64,128]{2,1,0:T(8,128)(2,1)S(1)}, bf16[80,2,256,256]{3,2,1,0:T(8,128)(2,1)}) custom-call(s32[1]{0:T(128)} %bitcast.at_y, s32[1]{0:T(128)} %bitcast.1.at_z, s32[80]{0:T(128)} %bitcast.35, bf16[80,256,128]{2,1,0:T(8,128)(2,1)} %bitcast.29, ...), custom_call_target="tpu_custom_call" | custom-call | flops 2000000000 | bytes 32000000 | tf_op jit(solution)/shard_map/box_density/pallas_call | solution.py:198
  19.8 3.6 %collective-permute-start = (bf16[8,64,128]{2,1,0:T(8,128)(2,1)S(1)}, bf16[8,64,128]{2,1,0:T(8,128)(2,1)S(1)}, u32[]{:S(2)}, u32[]{:S(2)}) collective-permute-start(bf16[8,64,128]{2,1,0:T(8,128)(2,1)S(1)} %get-tuple-element.7), channel_id=1, source_target_pairs={{0,7},{1,0},{2,1},{3,2},{4,3},{5,4},{6,5},{7,6},{8,15},{9,8},{10,9... | collective-permute-start | bytes 393224 | tf_op jit(solution)/shard_map/ppermute | solution.py:383
  23.4 0.0 collective-permute-start.1
  23.4 2.5 %collective-permute-done = bf16[8,64,128]{2,1,0:T(8,128)(2,1)S(1)} collective-permute-done((bf16[8,64,128]{2,1,0:T(8,128)(2,1)S(1)}, bf16[8,64,128]{2,1,0:T(8,128)(2,1)S(1)}, u32[]{:S(2)}, u32[]{:S(2)}) %collective-permute-start) | collective-permute-done | bytes 131104 | tf_op jit(solution)/shard_map/ppermute | solution.py:383
  25.9 3.1 %collective-permute-done.1 = bf16[8,64,128]{2,1,0:T(8,128)(2,1)S(1)} collective-permute-done((bf16[8,64,128]{2,1,0:T(8,128)(2,1)S(1)}, bf16[8,64,128]{2,1,0:T(8,128)(2,1)S(1)}, u32[]{:S(2)}, u32[]{:S(2)}) %collective-permute-start.1) | collective-permute-done | bytes 131104 | tf_op jit(solution)/shard_map/ppermute | solution.py:383
  29.0 0.1 add_convert_fusion
  29.1 3.1 %collective-permute-start.2 = (bf16[4,64,128]{2,1,0:T(8,128)(2,1)S(1)}, bf16[4,64,128]{2,1,0:T(8,128)(2,1)S(1)}, u32[]{:S(2)}, u32[]{:S(2)}) collective-permute-start(bf16[4,64,128]{2,1,0:T(8,128)(2,1)S(1)} %slice.9), channel_id=1, source_target_pairs={{0,24},{8,0},{16,8},{24,16},{1,25},{9,1},{17,9},{25,17},{2,26},{10... | collective-permute-start | bytes 196616 | tf_op jit(solution)/shard_map/ppermute | solution.py:383
  32.1 0.0 copy-done
  32.1 0.0 copy-done.2
  32.2 0.0 copy-done.3
  32.2 0.4 kernel_order.1
  32.6 1.5 %collective-permute-done.2 = bf16[4,64,128]{2,1,0:T(8,128)(2,1)S(1)} collective-permute-done((bf16[4,64,128]{2,1,0:T(8,128)(2,1)S(1)}, bf16[4,64,128]{2,1,0:T(8,128)(2,1)S(1)}, u32[]{:S(2)}, u32[]{:S(2)}) %collective-permute-start.2) | collective-permute-done | bytes 65568 | tf_op jit(solution)/shard_map/ppermute | solution.py:383
  34.1 2.8 %collective-permute-start.5 = (bf16[5,64,128]{2,1,0:T(8,128)(2,1)S(1)}, bf16[5,64,128]{2,1,0:T(8,128)(2,1)S(1)}, u32[]{:S(2)}, u32[]{:S(2)}) collective-permute-start(bf16[5,64,128]{2,1,0:T(8,128)(2,1)S(1)} %pad_maximum_fusion.1.refs_0_), channel_id=1, source_target_pairs={{0,96},{32,0},{64,32},{96,64},{1,97},{33,1},{65,33},{97,65},{2,98}... | collective-permute-start | bytes 245768 | tf_op jit(solution)/shard_map/ppermute | solution.py:383
  36.9 0.8 %collective-permute-start.4 = (bf16[5,64,128]{2,1,0:T(8,128)(2,1)S(1)}, bf16[5,64,128]{2,1,0:T(8,128)(2,1)S(1)}, u32[]{:S(2)}, u32[]{:S(2)}) collective-permute-start(bf16[5,64,128]{2,1,0:T(8,128)(2,1)S(1)} %pad_maximum_fusion.1.refs_0_), channel_id=1, source_target_pairs={{0,64},{32,96},{64,0},{96,32},{1,65},{33,97},{65,1},{97,33},{2,66}... | collective-permute-start | bytes 245768 | tf_op jit(solution)/shard_map/ppermute | solution.py:383
  37.7 0.9 %collective-permute-start.3 = (bf16[5,64,128]{2,1,0:T(8,128)(2,1)S(1)}, bf16[5,64,128]{2,1,0:T(8,128)(2,1)S(1)}, u32[]{:S(2)}, u32[]{:S(2)}) collective-permute-start(bf16[5,64,128]{2,1,0:T(8,128)(2,1)S(1)} %pad_maximum_fusion.1.refs_0_), channel_id=1, source_target_pairs={{0,32},{32,64},{64,96},{96,0},{1,33},{33,65},{65,97},{97,1},{2,34}... | collective-permute-start | bytes 245768 | tf_op jit(solution)/shard_map/ppermute | solution.py:383
  38.6 0.4 collective-permute-done.5.refs_3_
  39.0 3.9 %collective-permute-done.4.refs_2_ = bf16[5,64,128]{2,1,0:T(8,128)(2,1)S(1)} collective-permute-done((bf16[5,64,128]{2,1,0:T(8,128)(2,1)S(1)}, bf16[5,64,128]{2,1,0:T(8,128)(2,1)S(1)}, u32[]{:S(2)}, u32[]{:S(2)}) %collective-permute-start.4) | collective-permute-done | bytes 81952 | tf_op jit(solution)/shard_map/ppermute | solution.py:383
  42.9 0.8 %collective-permute-done.3.refs_1_ = bf16[5,64,128]{2,1,0:T(8,128)(2,1)S(1)} collective-permute-done((bf16[5,64,128]{2,1,0:T(8,128)(2,1)S(1)}, bf16[5,64,128]{2,1,0:T(8,128)(2,1)S(1)}, u32[]{:S(2)}, u32[]{:S(2)}) %collective-permute-start.3) | collective-permute-done | bytes 81952 | tf_op jit(solution)/shard_map/ppermute | solution.py:383
  43.8 1.0 %collective-permute-start.6 = (bf16[4,64,128]{2,1,0:T(8,128)(2,1)S(1)}, bf16[4,64,128]{2,1,0:T(8,128)(2,1)S(1)}, u32[]{:S(2)}, u32[]{:S(2)}) collective-permute-start(bf16[4,64,128]{2,1,0:T(8,128)(2,1)S(1)} %potential.1.pot), channel_id=1, source_target_pairs={{0,8},{8,16},{16,24},{24,0},{1,9},{9,17},{17,25},{25,1},{2,10},{10... | collective-permute-start | bytes 196616 | tf_op jit(solution)/shard_map/ppermute | solution.py:383
  44.8 4.9 %collective-permute-done.6 = bf16[4,64,128]{2,1,0:T(8,128)(2,1)S(1)} collective-permute-done((bf16[4,64,128]{2,1,0:T(8,128)(2,1)S(1)}, bf16[4,64,128]{2,1,0:T(8,128)(2,1)S(1)}, u32[]{:S(2)}, u32[]{:S(2)}) %collective-permute-start.6) | collective-permute-done | bytes 65568 | tf_op jit(solution)/shard_map/ppermute | solution.py:383
  49.7 0.0 collective-permute-start.8
  49.7 0.5 collective-permute-start.7
  50.2 0.3 natural_order.1
  50.6 0.7 copy.17
  51.2 1.0 %collective-permute-done.8.pot2 = bf16[8,64,128]{2,1,0:T(8,128)(2,1)S(1)} collective-permute-done((bf16[8,64,128]{2,1,0:T(8,128)(2,1)S(1)}, bf16[8,64,128]{2,1,0:T(8,128)(2,1)S(1)}, u32[]{:S(2)}, u32[]{:S(2)}) %collective-permute-start.8) | collective-permute-done | bytes 131104 | tf_op jit(solution)/shard_map/ppermute | solution.py:383
  52.2 3.1 %collective-permute-done.7.pot0 = bf16[8,64,128]{2,1,0:T(8,128)(2,1)S(1)} collective-permute-done((bf16[8,64,128]{2,1,0:T(8,128)(2,1)S(1)}, bf16[8,64,128]{2,1,0:T(8,128)(2,1)S(1)}, u32[]{:S(2)}, u32[]{:S(2)}) %collective-permute-start.7) | collective-permute-done | bytes 131104 | tf_op jit(solution)/shard_map/ppermute | solution.py:383
  55.3 0.0 copy-done.1
  55.3 0.0 copy-done.4
  55.3 11.5 %box_apply.1 = bf16[80,256,128]{2,1,0:T(8,128)(2,1)} custom-call(s32[1]{0:T(128)} %bitcast.at_y, s32[1]{0:T(128)} %bitcast.1.at_z, s32[80]{0:T(128)} %bitcast.36, bf16[8,64,128]{2,1,0:T(8,128)(2,1)S(1)} %collective-permute-done.7.pot0, bf16[8,64,128]{2,1,0:T(8,128)(2,1)S(1)} %pad_maximum_fusion.pot1, bf16[8,64,128]{2,1,0:T(8,128)(2,1)S(1)} %collective-permute-done.8.pot2, ...), custom_call_target="tpu_custom_call" | custom-call | flops 1000000000 | bytes 27000000 | tf_op jit(solution)/shard_map/box_apply/pallas_call | solution.py:315
  (5 shorter events, 0.1 us)
Async XLA Ops:
  0.6 31.5 %copy-start = (f32[128,128]{1,0:T(8,128)S(1)}, f32[128,128]{1,0:T(8,128)}, u32[]{:S(2)}) copy-start(f32[128,128]{1,0:T(8,128)} %constant.30.clone.cols) | copy-start | bytes 196612
  0.6 31.5 %copy-start.2 = (f32[64,64]{1,0:T(8,128)S(1)}, f32[64,64]{1,0:T(8,128)}, u32[]{:S(2)}) copy-start(f32[64,64]{1,0:T(8,128)} %constant.29.clone.rows) | copy-start | bytes 49156
  0.7 31.5 %copy-start.3 = (f32[1,8192]{1,0:T(1,128)S(1)}, f32[1,8192]{1,0:T(1,128)}, u32[]{:S(2)}) copy-start(f32[1,8192]{1,0:T(1,128)} %param.18) | copy-start | bytes 98308
  0.7 54.7 %copy-start.1 = (bf16[256,256]{1,0:T(8,128)(2,1)S(1)}, bf16[256,256]{1,0:T(8,128)(2,1)}, u32[]{:S(2)}) copy-start(bf16[256,256]{1,0:T(8,128)(2,1)} %constant.32.clone.wide_t) | copy-start | bytes 393220
  0.7 54.7 %copy-start.4 = (bf16[64,64]{1,0:T(8,128)(2,1)S(1)}, bf16[64,64]{1,0:T(8,128)(2,1)}, u32[]{:S(2)}) copy-start(bf16[64,64]{1,0:T(8,128)(2,1)} %constant.31.clone.odd_xt) | copy-start | bytes 24580
  19.8 6.1 %collective-permute-start = (bf16[8,64,128]{2,1,0:T(8,128)(2,1)S(1)}, bf16[8,64,128]{2,1,0:T(8,128)(2,1)S(1)}, u32[]{:S(2)}, u32[]{:S(2)}) collective-permute-start(bf16[8,64,128]{2,1,0:T(8,128)(2,1)S(1)} %get-tuple-element.7), channel_id=1, source_target_pairs={{0,7},{1,0},{2,1},{3,2},{4,3},{5,4},{6,5},{7,6},{8,15},{9,8},{10,9... | collective-permute-start | bytes 393224 | tf_op jit(solution)/shard_map/ppermute | solution.py:383
  23.4 5.6 %collective-permute-start.1 = (bf16[8,64,128]{2,1,0:T(8,128)(2,1)S(1)}, bf16[8,64,128]{2,1,0:T(8,128)(2,1)S(1)}, u32[]{:S(2)}, u32[]{:S(2)}) collective-permute-start(bf16[8,64,128]{2,1,0:T(8,128)(2,1)S(1)} %get-tuple-element.8), channel_id=1, source_target_pairs={{0,1},{1,2},{2,3},{3,4},{4,5},{5,6},{6,7},{7,0},{8,9},{9,10},{10,1... | collective-permute-start | bytes 393224 | tf_op jit(solution)/shard_map/ppermute | solution.py:383
  29.1 5.0 %collective-permute-start.2 = (bf16[4,64,128]{2,1,0:T(8,128)(2,1)S(1)}, bf16[4,64,128]{2,1,0:T(8,128)(2,1)S(1)}, u32[]{:S(2)}, u32[]{:S(2)}) collective-permute-start(bf16[4,64,128]{2,1,0:T(8,128)(2,1)S(1)} %slice.9), channel_id=1, source_target_pairs={{0,24},{8,0},{16,8},{24,16},{1,25},{9,1},{17,9},{25,17},{2,26},{10... | collective-permute-start | bytes 196616 | tf_op jit(solution)/shard_map/ppermute | solution.py:383
  34.1 4.9 %collective-permute-start.5 = (bf16[5,64,128]{2,1,0:T(8,128)(2,1)S(1)}, bf16[5,64,128]{2,1,0:T(8,128)(2,1)S(1)}, u32[]{:S(2)}, u32[]{:S(2)}) collective-permute-start(bf16[5,64,128]{2,1,0:T(8,128)(2,1)S(1)} %pad_maximum_fusion.1.refs_0_), channel_id=1, source_target_pairs={{0,96},{32,0},{64,32},{96,64},{1,97},{33,1},{65,33},{97,65},{2,98}... | collective-permute-start | bytes 245768 | tf_op jit(solution)/shard_map/ppermute | solution.py:383
  36.9 6.0 %collective-permute-start.4 = (bf16[5,64,128]{2,1,0:T(8,128)(2,1)S(1)}, bf16[5,64,128]{2,1,0:T(8,128)(2,1)S(1)}, u32[]{:S(2)}, u32[]{:S(2)}) collective-permute-start(bf16[5,64,128]{2,1,0:T(8,128)(2,1)S(1)} %pad_maximum_fusion.1.refs_0_), channel_id=1, source_target_pairs={{0,64},{32,96},{64,0},{96,32},{1,65},{33,97},{65,1},{97,33},{2,66}... | collective-permute-start | bytes 245768 | tf_op jit(solution)/shard_map/ppermute | solution.py:383
  37.7 6.0 %collective-permute-start.3 = (bf16[5,64,128]{2,1,0:T(8,128)(2,1)S(1)}, bf16[5,64,128]{2,1,0:T(8,128)(2,1)S(1)}, u32[]{:S(2)}, u32[]{:S(2)}) collective-permute-start(bf16[5,64,128]{2,1,0:T(8,128)(2,1)S(1)} %pad_maximum_fusion.1.refs_0_), channel_id=1, source_target_pairs={{0,32},{32,64},{64,96},{96,0},{1,33},{33,65},{65,97},{97,1},{2,34}... | collective-permute-start | bytes 245768 | tf_op jit(solution)/shard_map/ppermute | solution.py:383
  43.8 5.9 %collective-permute-start.6 = (bf16[4,64,128]{2,1,0:T(8,128)(2,1)S(1)}, bf16[4,64,128]{2,1,0:T(8,128)(2,1)S(1)}, u32[]{:S(2)}, u32[]{:S(2)}) collective-permute-start(bf16[4,64,128]{2,1,0:T(8,128)(2,1)S(1)} %potential.1.pot), channel_id=1, source_target_pairs={{0,8},{8,16},{16,24},{24,0},{1,9},{9,17},{17,25},{25,1},{2,10},{10... | collective-permute-start | bytes 196616 | tf_op jit(solution)/shard_map/ppermute | solution.py:383
  49.7 2.5 %collective-permute-start.8 = (bf16[8,64,128]{2,1,0:T(8,128)(2,1)S(1)}, bf16[8,64,128]{2,1,0:T(8,128)(2,1)S(1)}, u32[]{:S(2)}, u32[]{:S(2)}) collective-permute-start(bf16[8,64,128]{2,1,0:T(8,128)(2,1)S(1)} %pad_maximum_fusion.pot1), channel_id=1, source_target_pairs={{0,7},{1,0},{2,1},{3,2},{4,3},{5,4},{6,5},{7,6},{8,15},{9,8},{10,9... | collective-permute-start | bytes 393224 | tf_op jit(solution)/shard_map/ppermute | solution.py:383
  49.7 5.6 %collective-permute-start.7 = (bf16[8,64,128]{2,1,0:T(8,128)(2,1)S(1)}, bf16[8,64,128]{2,1,0:T(8,128)(2,1)S(1)}, u32[]{:S(2)}, u32[]{:S(2)}) collective-permute-start(bf16[8,64,128]{2,1,0:T(8,128)(2,1)S(1)} %pad_maximum_fusion.pot1), channel_id=1, source_target_pairs={{0,1},{1,2},{2,3},{3,4},{4,5},{5,6},{6,7},{7,0},{8,9},{9,10},{10,1... | collective-permute-start | bytes 393224 | tf_op jit(solution)/shard_map/ppermute | solution.py:383
